TPU v7x, 32 devices: a whole 2x2x4 slice. The times are simulated.
32 devices in a mesh: tm: 4 (over x, core), freq: 8 (over z, y).
Axes of the slice: x: 2, y: 2, z: 4, core: 2. Of those that a mesh axis runs over, the one named last changes fastest.
Arguments:
- voltages: bfloat16 [4, 1024, 258048], P('tm', 'freq'), may hold values from -6 to 6
- chan_bins: int32 [32], replicated, may hold values from 0 to 2047, as said below
- antenna_map: int32 [1024], replicated, may hold values from 0 to 1023, each once
- beam_index: int32 [512], replicated, may hold values from 0 to 511, each once
- delays: float32 [512, 1024], replicated, may hold values from -4 to 4
Outputs:
- visibilities: float32 [32, 2, 1024, 1024], P(('tm', 'freq'))
- beam_volts: float32 [512, 32, 2, 192], P('freq', 'tm')
Inputs may be any that keep to these rules, and one draw needn't show every extreme that they name: `chan_bins`: the 32 bins are distinct, below 2048. `antenna_map`: each signal feeds exactly one antenna input. `beam_index`: each beam has a pointing of its own.
All inputs are finite; a program needn't handle non-finite values.
Results may differ from a plain program's by a relative error of at most 0.006.
Values may be sent and summed in bfloat16 or wider, within the bound.
No kernel may reach another device: no remote copies, remote signals or barrier semaphores. Data moves between devices by JAX's collectives and lax.ppermute only.
A program may use at most 256 MiB of HBM per device.

v0:
```python
import math

import jax
import jax.numpy as jnp
from jax import lax
from jax.sharding import PartitionSpec as P

NFFT = 4096
TAPS = 16


def prototype(tap_count, length):
    total = tap_count * length
    offsets = jnp.arange(total, dtype=jnp.float32)
    shifted = (offsets - 0.5 * total + 0.5) / length
    window = 0.5 - 0.5 * jnp.cos(2.0 * math.pi / total * (offsets + 0.5))
    return (jnp.sinc(shifted) * window).reshape(tap_count, length)


def dft_table(bins, length):
    positions = jnp.arange(length, dtype=jnp.int32)
    products = bins[:, None] * positions[None, :] % length
    angles = products.astype(jnp.float32) * (2.0 * math.pi / length)
    scale = 1.0 / math.sqrt(length)
    return jnp.stack([jnp.cos(angles) * scale, -jnp.sin(angles) * scale]).astype(jnp.bfloat16)


def filter_bank(samples, taps_table, frames):
    total = jnp.zeros((samples.shape[0], frames, samples.shape[2]), jnp.float32)
    for tap_index in range(taps_table.shape[0]):
        total = total + taps_table[tap_index] * samples[
            :, tap_index : tap_index + frames, :
        ].astype(jnp.float32)
    return total.astype(jnp.bfloat16)


def body(voltages, chan_bins, antenna_map, beam_index, delays):
    signals_dev = voltages.shape[1]
    frames = voltages.shape[2] // NFFT - TAPS + 1
    channels = chan_bins.shape[0]
    tm_count = lax.axis_size("tm")
    freq_count = lax.axis_size("freq")
    taps_table = prototype(TAPS, NFFT)
    table = dft_table(chan_bins, NFFT)
    samples = voltages[0].reshape(signals_dev, frames + TAPS - 1, NFFT)
    filtered = filter_bank(samples, taps_table, frames).reshape(signals_dev * frames, NFFT)
    spectra = jnp.einsum("rcn,mn->crm", table, filtered, preferred_element_type=jnp.float32)
    spectra = spectra.astype(jnp.bfloat16).reshape(channels, 2, signals_dev, frames)
    moved = lax.all_to_all(
        spectra[:, :, None], ("tm", "freq"), split_axis=0, concat_axis=2, tiled=True
    )
    moved = moved.reshape(2, tm_count, freq_count, signals_dev, frames).transpose(0, 2, 3, 1, 4)
    moved = moved.reshape(2, freq_count * signals_dev, tm_count * frames)
    volts = jnp.take(moved, antenna_map, axis=1)
    swapped = jnp.stack([volts[1], -volts[0]])
    real_part = jnp.einsum("rat,rbt->ab", volts, volts, preferred_element_type=jnp.float32)
    imag_part = jnp.einsum("rat,rbt->ab", swapped, volts, preferred_element_type=jnp.float32)
    visibilities = jnp.stack([real_part, imag_part]) / volts.shape[2]
    channel = lax.axis_index("tm") * freq_count + lax.axis_index("freq")
    bin_value = lax.dynamic_index_in_dim(chan_bins, channel, keepdims=False)
    selected = jnp.take(delays, beam_index, axis=0)
    phase = selected * bin_value.astype(jnp.float32) * (2.0 * math.pi / NFFT)
    cosine = jnp.cos(phase).astype(jnp.bfloat16)
    sine = jnp.sin(phase).astype(jnp.bfloat16)
    weights = jnp.stack([jnp.stack([cosine, sine], 1), jnp.stack([-sine, cosine], 1)])
    formed = jnp.einsum("obra,rat->bot", weights, volts, preferred_element_type=jnp.float32)
    formed = formed * (1.0 / math.sqrt(volts.shape[1]))
    turned = lax.all_to_all(formed[:, None], "freq", split_axis=0, concat_axis=1, tiled=True)
    return (visibilities[None], turned)


def solution(mesh):
    return jax.shard_map(
        body,
        mesh=mesh,
        in_specs=(P("tm", "freq", None), P(), P(), P(), P()),
        out_specs=(P(("tm", "freq"), None, None, None), P("freq", "tm", None, None)),
        check_vma=False,
    )
```

profile of v0, /device:TPU:0, one launch (start us, length us, event | category | flops | bytes accessed | tf_op | source)
XLA Modules:
  0.0 568.9 jit_solution(13914067962926165342)
XLA Ops:
  0.6 0.0 copy-start
  0.6 1.2 fusion.35
  1.9 76.4 %copy.21 = bf16[1,128,258048]{1,2,0:T(8,128)(2,1)} copy(bf16[1,128,258048]{2,1,0:T(8,128)(2,1)} %param.5) | data formatting | bytes 132120576 | tf_op args[0]
  78.3 308.5 %add_convert_fusion = bf16[128,48,4096]{0,2,1:T(8,128)(2,1)} fusion(bf16[128,63,4096]{0,2,1:T(8,128)(2,1)} %bitcast.70, f32[4096]{0:T(1024)S(1)} %get-tuple-element.15, f32[4096]{0:T(1024)S(1)} %get-tuple-element.16, f32[4096]{0:T(1024)S(1)} %get-tuple-element.17, f32[4096]{0:T(1024)S(1)} %get-tuple-element.18, f32[4096]{0:T(1024)S(1)} %get-tuple-element.19, ...), kind=kLoop, calls=%fused_computation.2 | loop fusion | flops 1207959552 | bytes 855900160 | tf_op jit(solution)/shard_map/convert_element_type | solution.py:34
  386.8 0.0 copy-start.4
  386.8 61.3 %copy.22 = bf16[128,48,4096]{2,1,0:T(8,128)(2,1)} copy(bf16[128,48,4096]{0,2,1:T(8,128)(2,1)} %add_convert_fusion) | data formatting | bytes 100663296 | tf_op jit(solution)/shard_map/convert_element_type | solution.py:34
  448.1 2.5 multiply_convert_fusion.1
  450.6 23.8 %fusion = bf16[32,2,6144]{2,0,1:T(8,128)(2,1)S(1)} fusion(bf16[6144,4096,1]{1,0,2:T(8,128)(2,1)} %bitcast.71, bf16[1,32,4096]{2,1,0:T(8,128)(2,1)S(1)} %get-tuple-element.31, bf16[1,32,4096]{2,1,0:T(8,128)(2,1)S(1)} %get-tuple-element.30), kind=kOutput, calls=%fused_computation.5 | convolution fusion | flops 3222667264 | bytes 51642368 | tf_op jit(solution)/shard_map/rcn,mn->crm/dot_general | solution.py:47
  474.4 3.1 broadcast_in_dim_reshape.3
  477.6 2.6 copy.23
  480.2 7.5 %all-to-all-start = ((bf16[32,2,1,128,48]{3,4,2,1,0:T(8,128)(2,1)}), bf16[32,2,1,128,48]{3,4,2,1,0:T(8,128)(2,1)S(1)}, u32[]{:S(2)}, u32[]{:S(2)}) async-start(bf16[32,2,1,128,48]{3,4,2,1,0:T(8,128)(2,1)} %copy.23), calls=%async_computation | async-start | bytes 1572864 | tf_op jit(solution)/shard_map/all_to_all | solution.py:49
  487.7 0.6 dynamic_slice.4
  489.0 2.7 gather_fusion.1
  491.7 8.5 %cosine_convert_fusion = bf16[512,1,1024]{2,0,1:T(8,128)(2,1)S(1)} fusion(f32[512,1024]{1,0:T(8,128)} %gather_fusion.1, f32[]{:T(128)} %bitcast.15, pred[512]{0:T(512)(128)(4,1)S(1)} %compare_and_fusion.1), kind=kLoop, calls=%fused_computation.18 | loop fusion | flops 2097152 | bytes 3146244 | tf_op jit(solution)/shard_map/convert_element_type | solution.py:63
  500.2 8.8 %fusion.65 = (bf16[512,1,1024]{2,0,1:T(8,128)(2,1)S(1)}, bf16[512,1,1024]{2,0,1:T(8,128)(2,1)S(1)}) fusion(f32[]{:T(128)} %bitcast.15, f32[512,1024]{1,0:T(8,128)} %gather_fusion.1, pred[512]{0:T(512)(128)(4,1)S(1)} %compare_and_fusion.1), kind=kLoop, calls=%fused_computation.92 | loop fusion | flops 3670016 | bytes 4194820 | tf_op jit(solution)/shard_map/neg | solution.py:65
  509.0 2.4 maximum_bitcast_fusion
  511.4 1.2 copy.32
  512.6 2.2 reshape.294
  514.8 2.5 copy.25
  517.2 8.5 %gather_fusion = bf16[1024,2,192]{2,1,0:T(2,128)(2,1)} fusion(bf16[2,1024,192]{2,0,1:T(2,128)(2,1)S(1)} %copy.25, s32[1024]{0:T(1024)S(1)} %fusion.60), kind=kCustom, calls=%fused_computation | custom fusion | bytes 1576960 | tf_op jit(solution)/shard_map/jit(_take)/gather | solution.py:54
  525.7 2.4 copy.26
  528.2 4.9 fusion.13
  533.1 2.2 copy.27
  535.3 5.6 all-to-all-start.1
  540.9 1.2 fusion.20
  542.1 0.1 fusion.66
  542.2 1.3 convolution_bitcast_fusion
  543.5 1.3 convolution_bitcast_fusion.1
  544.8 4.4 maximum_multiply_fusion
  549.2 17.8 %all-to-all-done.1 = f32[512,1,2,192]{3,2,1,0:T(2,128)S(1)} async-done(((f32[512,1,2,192]{3,2,1,0:T(2,128)}), f32[512,1,2,192]{3,2,1,0:T(2,128)S(1)}, u32[]{:S(2)}, u32[]{:S(2)}) %all-to-all-start.1) | async-done | bytes 786464 | tf_op jit(solution)/shard_map/all_to_all | solution.py:68
  567.0 0.1 copy.28
  567.1 1.8 copy.29
  (15 shorter events, 0.1 us)
Async XLA Ops:
  0.6 488.4 %copy-start = (f32[512,1024]{1,0:T(8,128)S(1)}, f32[512,1024]{1,0:T(8,128)}, u32[]{:S(2)}) copy-start(f32[512,1024]{1,0:T(8,128)} %param.9) | copy-start | bytes 6291460
  386.8 61.3 %copy-start.4 = (s32[32]{0:T(128)S(1)}, s32[32]{0:T(128)}, u32[]{:S(2)}) copy-start(s32[32]{0:T(128)} %param.6) | copy-start | bytes 388
  448.1 40.9 %copy-start.3 = (s32[512]{0:T(512)S(1)}, s32[512]{0:T(512)}, u32[]{:S(2)}) copy-start(s32[512]{0:T(512)} %param.8) | copy-start | bytes 6148
  450.6 60.8 %copy-start.2 = (s32[1024]{0:T(1024)S(1)}, s32[1024]{0:T(1024)}, u32[]{:S(2)}) copy-start(s32[1024]{0:T(1024)} %param.7) | copy-start | bytes 12292
  480.2 31.2 %all-to-all-start = ((bf16[32,2,1,128,48]{3,4,2,1,0:T(8,128)(2,1)}), bf16[32,2,1,128,48]{3,4,2,1,0:T(8,128)(2,1)S(1)}, u32[]{:S(2)}, u32[]{:S(2)}) async-start(bf16[32,2,1,128,48]{3,4,2,1,0:T(8,128)(2,1)} %copy.23), calls=%async_computation | async-start | bytes 1572864 | tf_op jit(solution)/shard_map/all_to_all | solution.py:49
  528.1 7.2 %copy-start.1 = (bf16[1024,2,192]{0,2,1:T(8,128)(2,1)}, bf16[1024,2,192]{0,2,1:T(8,128)(2,1)S(1)}, u32[]{:S(2)}) copy-start(bf16[1024,2,192]{0,2,1:T(8,128)(2,1)S(1)} %copy.26) | copy-start | bytes 2359300
  535.3 31.7 %all-to-all-start.1 = ((f32[512,1,2,192]{3,2,1,0:T(2,128)}), f32[512,1,2,192]{3,2,1,0:T(2,128)S(1)}, u32[]{:S(2)}, u32[]{:S(2)}) async-start(f32[512,1,2,192]{3,2,1,0:T(2,128)} %copy.27), calls=%async_computation.1 | async-start | bytes 2097152 | tf_op jit(solution)/shard_map/all_to_all | solution.py:68
where the time goes:
time: 573 us; the launch traced here: 569 us
  other arithmetic  338 us (59%)
  local copies, waits for them, and re-layouts  168 us (29%)
  matrix products  31.3 us (5%)
  waiting for transfers between devices  17.8 us (3%)
  starting transfers between devices  13.1 us (2%)
    convert_element_type x1, other arithmetic, filter_bank(): return total.astype(jnp.bfloat16)  308 us
    unnamed x12, local copies, waits for them, and re-layouts  78.2 us
    convert_element_type x1, local copies, waits for them, and re-layouts, filter_bank(): return total.astype(jnp.bfloat16)  61.3 us
    dot_general x1, matrix products, body(): jnp.einsum('rcn,mn->crm', table, filtered, preferred_element_type=jnp.flo...  23.8 us
    all_to_all x1, waiting for transfers between devices, body(): lax.all_to_all(formed[:, None], 'freq', split_axis=0, concat_axis=1, tile...  17.8 us
  transfers between devices with their start and end apart: 2, of which 1 were waited for; matrix products, arithmetic and copies ran while one was open for 5% of the time, Pallas kernels for 0%

commit v1 on v0

v1 whole, which is shorter than its diff:
```python
import functools
import math

import jax
import jax.numpy as jnp
import numpy as np
from jax import lax
from jax.experimental import pallas as pl
from jax.experimental.pallas import tpu as pltpu
from jax.sharding import PartitionSpec as P

NFFT = 4096
TAPS = 16
RANK = 8
LANES = 128
NT = (((1,), (1,)), ((), ()))


def taps_factors():
    total = TAPS * NFFT
    offsets = np.arange(total, dtype=np.float64)
    shifted = (offsets - 0.5 * total + 0.5) / NFFT
    window = 0.5 - 0.5 * np.cos(2.0 * np.pi / total * (offsets + 0.5))
    taps = (np.sinc(shifted) * window).reshape(TAPS, NFFT)
    left, _, _ = np.linalg.svd(taps, full_matrices=False)
    mix = np.round(left[:, :RANK], 7)
    parity = []
    for r in range(RANK):
        sign = 1.0 if np.sum(mix[:, r] * mix[::-1, r]) > 0 else -1.0
        mix[:, r] = 0.5 * (mix[:, r] + sign * mix[::-1, r])
        parity.append(sign)
    gram = np.sum(mix[:, :, None] * mix[:, None, :], axis=0)
    inverse = np.linalg.inv(gram)
    basis = np.zeros((RANK, NFFT))
    for r in range(RANK):
        dual = np.sum(mix * inverse[r], axis=1)
        basis[r] = np.sum(dual[:, None] * taps, axis=0)
    return mix, basis, parity


def term_tiles(parity, per_tile):
    tiles = []
    for wanted in (1.0, -1.0):
        group = [r for r in range(RANK) if parity[r] == wanted]
        for at in range(0, len(group), per_tile):
            tiles.append((tuple(group[at : at + per_tile]), wanted))
    return tiles


def cos_turns(turns):
    rest = 0.25 - jnp.abs(turns - jnp.round(turns))
    angle = rest * (2.0 * math.pi)
    square = angle * angle
    total = -1.0 / math.factorial(11) + square * (1.0 / math.factorial(13))
    for power in (9, 7, 5, 3):
        total = (-1.0) ** (power // 2) / math.factorial(power) + square * total
    return angle + angle * square * total


def spectra_kernel(chunk, chunks_per_step, frames, width, signs,
                   x_ref, w_ref, mix_ref, out_ref, y_ref, acc_ref, turned_ref):
    step = pl.program_id(0)
    signals = x_ref.shape[0]
    columns = w_ref.shape[1]
    lag = (TAPS - 1 + chunk - 1) // chunk + 1
    size = min(width, LANES)
    out_tiles = width // size
    per_tile = LANES // size

    def combine(first, slot):
        for out_tile in range(out_tiles):
            for row in range(0, signals, 8):
                totals = [jnp.zeros((8, LANES), jnp.float32) for _ in range(chunk)]
                for tile in range(out_tile, columns // LANES, out_tiles):
                    held = [
                        y_ref[first + i, row : row + 8, tile * LANES : (tile + 1) * LANES]
                        for i in range(chunk + TAPS - 1)
                    ]
                    for k in range(TAPS // 2):
                        factor = mix_ref[tile, k]
                        for o in range(chunk):
                            low, high = held[o + k], held[o + TAPS - 1 - k]
                            both = low + high if signs[tile // out_tiles] > 0 else low - high
                            totals[o] = totals[o] + factor * both
                for o in range(chunk):
                    acc_ref[o, row : row + 8, :] = totals[o]
            for o in range(chunk):
                turned = acc_ref[o].T
                total = turned[:size]
                for i in range(1, per_tile):
                    total = total + turned[i * size : (i + 1) * size]
                turned_ref[slot * chunk + o, out_tile * size : (out_tile + 1) * size, :] = total

    def one_chunk(inner, carry):
        at = step * chunks_per_step + inner
        combine(jnp.maximum(at - lag, 0) * chunk, at)
        rows = jnp.concatenate(
            [
                x_ref[:, pl.ds(pl.multiple_of((inner * chunk + i) * NFFT, NFFT), NFFT)]
                for i in range(chunk)
            ],
            axis=0,
        )
        product = jnp.dot(rows, w_ref[...], preferred_element_type=jnp.float32)
        y_ref[pl.ds(at * chunk, chunk)] = product.reshape(chunk, signals, columns)
        return carry

    lax.fori_loop(0, chunks_per_step, one_chunk, 0)

    @pl.when(step == pl.num_programs(0) - 1)
    def _():
        chunks = (frames + TAPS - 1) // chunk

        def rest(group, carry):
            combine(group * chunk, group + lag)
            return carry

        lax.fori_loop(chunks - lag, frames // chunk, rest, 0)
        for row in range(width):
            out_ref[row] = turned_ref[pl.ds(lag * chunk, frames), row, :].astype(out_ref.dtype)


def spectra_of(samples, weights, mix, signs, frames):
    signals, length = samples.shape
    in_frames = length // NFFT
    columns = weights.shape[1]
    width = columns // RANK
    chunk = math.gcd(3, math.gcd(in_frames, frames))
    chunks = in_frames // chunk
    per_step = next(d for d in (3, 2, 1) if chunks % d == 0)
    lag = (TAPS - 1 + chunk - 1) // chunk + 1
    body = functools.partial(spectra_kernel, chunk, per_step, frames, width, signs)
    block = per_step * chunk * NFFT
    return pl.pallas_call(
        body,
        grid=(chunks // per_step,),
        in_specs=[
            pl.BlockSpec((signals, block), lambda i: (0, i)),
            pl.BlockSpec(weights.shape, lambda i: (0, 0), pipeline_mode=pl.Buffered(1)),
            pl.BlockSpec(mix.shape, lambda i: (0, 0, 0, 0), pipeline_mode=pl.Buffered(1)),
        ],
        out_specs=pl.BlockSpec((width, frames, signals), lambda i: (0, 0, 0)),
        out_shape=jax.ShapeDtypeStruct((width, frames, signals), jnp.bfloat16),
        scratch_shapes=[
            pltpu.VMEM((in_frames, signals, columns), jnp.float32),
            pltpu.VMEM((chunk, signals, LANES), jnp.float32),
            pltpu.VMEM((frames + lag * chunk, width, signals), jnp.float32),
        ],
        compiler_params=pltpu.CompilerParams(vmem_limit_bytes=60 << 20),
        cost_estimate=pl.CostEstimate(
            flops=2 * signals * length * columns,
            bytes_accessed=2 * signals * length,
            transcendentals=0,
        ),
        name="spectra",
    )(samples, weights, mix)


def steering_kernel(bin_ref, delays_ref, beams_ref, antennas_ref, table_ref, place_ref, raw_ref):
    pointings, antennas = delays_ref.shape
    beams = beams_ref.shape[1]
    rows = 32
    turn = bin_ref[0, 0]

    def some(at, carry):
        window = pl.ds(pl.multiple_of(at * rows, rows), rows)
        turns = delays_ref[window, :] * turn * (1.0 / NFFT)
        raw_ref[window, :antennas] = cos_turns(turns).astype(jnp.bfloat16)
        raw_ref[window, antennas:] = cos_turns(turns - 0.25).astype(jnp.bfloat16)
        return carry

    lax.fori_loop(0, pointings // rows, some, 0)
    column = jnp.broadcast_to(antennas_ref[...], (LANES, antennas)).T
    for tile in range(antennas // LANES):
        lanes = lax.broadcasted_iota(jnp.int32, (antennas, LANES), 1) + tile * LANES
        place_ref[:, tile * LANES : (tile + 1) * LANES] = jnp.where(
            column == lanes, 1.0, 0.0
        ).astype(jnp.bfloat16)
    wanted = jnp.broadcast_to(beams_ref[...], (LANES, beams)).T
    chosen = jnp.concatenate(
        [
            jnp.where(
                wanted == lax.broadcasted_iota(jnp.int32, (beams, LANES), 1) + tile * LANES, 1.0, 0.0
            ).astype(jnp.bfloat16)
            for tile in range(pointings // LANES)
        ],
        axis=1,
    )
    for part in range(2):
        ordered = jnp.dot(
            chosen, raw_ref[:, part * antennas : (part + 1) * antennas],
            preferred_element_type=jnp.float32,
        ).astype(jnp.bfloat16)
        table_ref[part] = jnp.dot(
            ordered, place_ref[...], preferred_element_type=jnp.float32
        ).astype(jnp.bfloat16)


def steering_of(bin_value, delays, beam_index, antenna_map):
    pointings, antennas = delays.shape
    beams = beam_index.shape[0]
    vmem = pl.BlockSpec(memory_space=pltpu.VMEM)
    return pl.pallas_call(
        steering_kernel,
        in_specs=[pl.BlockSpec(memory_space=pltpu.SMEM), vmem, vmem, vmem],
        out_specs=[vmem, vmem],
        out_shape=[
            jax.ShapeDtypeStruct((2, beams, antennas), jnp.bfloat16),
            jax.ShapeDtypeStruct((antennas, antennas), jnp.bfloat16),
        ],
        scratch_shapes=[pltpu.VMEM((pointings, 2 * antennas), jnp.bfloat16)],
        compiler_params=pltpu.CompilerParams(vmem_limit_bytes=32 << 20),
        cost_estimate=pl.CostEstimate(
            flops=40 * pointings * antennas + 4 * beams * antennas * (antennas + pointings),
            bytes_accessed=8 * pointings * antennas,
            transcendentals=0,
        ),
        name="steering",
    )(bin_value.reshape(1, 1), delays, beam_index.reshape(1, beams), antenna_map.reshape(1, antennas))


def series_of(moved):
    if len(moved.shape) == 3:
        real, imag = moved[0], moved[1]
    else:
        blocks, groups = moved.shape[:2]
        real, imag = (
            jnp.concatenate(
                [
                    jnp.concatenate([moved[q, f, part] for f in range(groups)], axis=1)
                    for q in range(blocks)
                ],
                axis=0,
            )
            for part in range(2)
        )
    return jnp.concatenate([real, imag], axis=0), jnp.concatenate([imag, -real], axis=0)


def beams_kernel(scale, moved_ref, table_ref, out_ref):
    straight, crossed = series_of(moved_ref)
    formed = lax.dot_general(table_ref[0], straight, NT, preferred_element_type=jnp.float32)
    formed += lax.dot_general(table_ref[1], crossed, NT, preferred_element_type=jnp.float32)
    formed = (formed * scale).astype(out_ref.dtype)
    out_ref[...] = formed.reshape(out_ref.shape)


def beams_of(moved, table, groups, times):
    _, beams, antennas = table.shape
    vmem = pl.BlockSpec(memory_space=pltpu.VMEM)
    return pl.pallas_call(
        functools.partial(beams_kernel, 1.0 / math.sqrt(antennas)),
        in_specs=[vmem, vmem],
        out_specs=vmem,
        out_shape=jax.ShapeDtypeStruct((groups, beams // groups, 2 * times), jnp.bfloat16),
        compiler_params=pltpu.CompilerParams(vmem_limit_bytes=32 << 20),
        name="beams",
    )(moved, table)


def visibility_kernel(moved_ref, place_ref, out_ref, straight_ref, crossed_ref):
    step = pl.program_id(0)
    rows = out_ref.shape[2]
    times = straight_ref.shape[1] // 2

    @pl.when(step == 0)
    def _():
        for wide, held in zip(series_of(moved_ref), (straight_ref, crossed_ref)):
            held[...] = lax.dot_general(
                place_ref[...], wide, NT, preferred_element_type=jnp.float32
            ).astype(jnp.bfloat16)

    window = pl.ds(pl.multiple_of(step * rows, rows), rows)
    for part, held in enumerate((straight_ref, crossed_ref)):
        out_ref[0, part] = lax.dot_general(
            held[window, :], straight_ref[...], NT, preferred_element_type=jnp.float32
        ) * (1.0 / times)


def visibilities_of(moved, place, times):
    antennas = place.shape[0]
    rows = antennas // 4
    return pl.pallas_call(
        visibility_kernel,
        grid=(antennas // rows,),
        in_specs=[
            pl.BlockSpec(moved.shape, lambda i: (0,) * len(moved.shape)),
            pl.BlockSpec(place.shape, lambda i: (0, 0)),
        ],
        out_specs=pl.BlockSpec((1, 2, rows, antennas), lambda i: (0, 0, i, 0)),
        out_shape=jax.ShapeDtypeStruct((1, 2, antennas, antennas), jnp.float32),
        scratch_shapes=[pltpu.VMEM((antennas, 2 * times), jnp.bfloat16)] * 2,
        compiler_params=pltpu.CompilerParams(vmem_limit_bytes=32 << 20),
        cost_estimate=pl.CostEstimate(
            flops=8 * antennas * antennas * 2 * times,
            bytes_accessed=8 * antennas * antennas,
            transcendentals=0,
        ),
        name="visibilities",
    )(moved, place)


def body(voltages, chan_bins, antenna_map, beam_index, delays):
    signals_dev = voltages.shape[1]
    frames = voltages.shape[2] // NFFT - TAPS + 1
    channels = chan_bins.shape[0]
    tm_count = lax.axis_size("tm")
    freq_count = lax.axis_size("freq")
    times = tm_count * frames

    mix, basis, parity = taps_factors()
    per_tile = max(1, LANES // (2 * channels))
    tiles = term_tiles(parity, per_tile)
    order = [r for terms, _ in tiles for r in terms]
    signs = tuple(sign for _, sign in tiles)
    lanes = np.repeat(mix[: TAPS // 2, order], 2 * channels, axis=1).astype(np.float32)
    lanes = lanes.reshape(TAPS // 2, -1, 1, LANES).transpose(1, 0, 2, 3)
    mix_lanes = jnp.broadcast_to(jnp.asarray(lanes), (lanes.shape[0], TAPS // 2, 8, LANES))

    positions = jnp.arange(NFFT, dtype=jnp.int32)
    products = positions[:, None] * jnp.repeat(chan_bins, 2)[None, :] % NFFT
    quarter = jnp.asarray(np.tile(np.array([0.0, 0.25], np.float32), channels))
    table = cos_turns(products.astype(jnp.float32) * (1.0 / NFFT) + quarter)
    table = (table * (1.0 / math.sqrt(NFFT))).astype(jnp.bfloat16).astype(jnp.float32)
    basis_columns = jnp.asarray(basis[order].T.astype(np.float32))
    weights = (basis_columns[:, :, None] * table[:, None, :]).astype(jnp.bfloat16)
    weights = weights.reshape(NFFT, RANK * 2 * channels)

    spectra = spectra_of(voltages[0], weights, mix_lanes, signs, frames)
    spectra = spectra.reshape(channels, 2, frames, signals_dev)
    moved = lax.all_to_all(spectra, ("tm", "freq"), split_axis=0, concat_axis=0, tiled=True)
    moved = moved.reshape(tm_count, freq_count, 2, frames, signals_dev)
    if signals_dev % LANES:
        moved = moved.transpose(2, 0, 3, 1, 4).reshape(2, times, freq_count * signals_dev)

    channel = lax.axis_index("tm") * freq_count + lax.axis_index("freq")
    bin_value = lax.dynamic_index_in_dim(chan_bins, channel, keepdims=False)
    table, place = steering_of(bin_value.astype(jnp.float32), delays, beam_index, antenna_map)
    formed = beams_of(moved, table, freq_count, times)
    turned = lax.all_to_all(formed, "freq", split_axis=0, concat_axis=0, tiled=True)
    visibilities = visibilities_of(moved, place, times)
    turned = turned.transpose(1, 0, 2).astype(jnp.float32)
    return (visibilities, turned.reshape(turned.shape[0], turned.shape[1], 2, times))


def solution(mesh):
    return jax.shard_map(
        body,
        mesh=mesh,
        in_specs=(P("tm", "freq", None), P(), P(), P(), P()),
        out_specs=(P(("tm", "freq"), None, None, None), P("freq", "tm", None, None)),
        check_vma=False,
    )
```

time: 573 us -> 122 us (0.21)
  other arithmetic: 338 us -> 5.65 us
  local copies, waits for them, and re-layouts: 168 us -> 15.4 us
  Pallas kernels: 0 us -> 74 us
  matrix products: 31.3 us -> 0 us
    convert_element_type x2, other arithmetic: 317 us -> 5.59 us  [the longest x1 3.67 us: body(): (basis_columns[:, :, None] * table[:, None, :]).astype(jnp.bfloat16)]
    pallas_call x0 -> x4, Pallas kernels: none -> 74 us  [the longest x1 58 us: spectra_of(): pl.pallas_call(body, grid=(chunks // per_step,), in_specs=[pl.BlockSpec((...]
    unnamed x12 -> x15, local copies, waits for them, and re-layouts: 78.2 us -> 6.06 us
    convert_element_type x1, local copies, waits for them, and re-layouts: 61.3 us -> 6.48 us  [body(): (basis_columns[:, :, None] * table[:, None, :]).astype(jnp.bfloat16)]
    dot_general x4 -> x0, matrix products: 31.3 us -> none  [the longest x1 23.8 us: body(): jnp.einsum('rcn,mn->crm', table, filtered, preferred_element_type=jnp.flo...]
    gather x3 -> x0, local copies, waits for them, and re-layouts: 13.6 us -> none  [the longest x2 10.9 us: body(): volts = jnp.take(moved, antenna_map, axis=1)]
    neg x1 -> x0, other arithmetic: 8.79 us -> none  [body(): -sine]
    another operation x2 -> x0, local copies, waits for them, and re-layouts: 5.77 us -> none  [body(): spectra[:, :, None]]
  transfers between devices with their start and end apart: 2 -> 2, of which waited for: 1 -> 2; matrix products, arithmetic and copies ran while one was open for 5% -> 0% of each run, Pallas kernels for 0% -> 12%
where the time goes in v1:
time: 122 us; the launch traced here: 121 us
  Pallas kernels  74 us (61%)
  local copies, waits for them, and re-layouts  15.4 us (13%)
  waiting for transfers between devices  13.7 us (11%)
  starting transfers between devices  10.9 us (9%)
  other arithmetic  5.65 us (5%)
  between operations  1.39 us (1%)
    pallas_call x1, Pallas kernels, spectra_of(): pl.pallas_call(body, grid=(chunks // per_step,), in_specs=[pl.BlockSpec((...  58 us
    all_to_all x1, waiting for transfers between devices, body(): lax.all_to_all(spectra, ('tm', 'freq'), split_axis=0, concat_axis=0, tile...  11 us
    all_to_all x1, starting transfers between devices, body(): lax.all_to_all(spectra, ('tm', 'freq'), split_axis=0, concat_axis=0, tile...  7.3 us
    pallas_call x1, Pallas kernels, visibilities_of(): pl.pallas_call(visibility_kernel, grid=(antennas // rows,), in_specs=[pl....  7.21 us
    pallas_call x1, Pallas kernels, steering_of(): pl.pallas_call(steering_kernel, in_specs=[pl.BlockSpec(memory_space=pltpu...  6.77 us
    convert_element_type x1, local copies, waits for them, and re-layouts, body(): (basis_columns[:, :, None] * table[:, None, :]).astype(jnp.bfloat16)  6.48 us
    unnamed x15, local copies, waits for them, and re-layouts  6.06 us
    convert_element_type x1, other arithmetic, body(): (basis_columns[:, :, None] * table[:, None, :]).astype(jnp.bfloat16)  3.67 us
  transfers between devices with their start and end apart: 2, of which 2 were waited for; matrix products, arithmetic and copies ran while one was open for 0% of the time, Pallas kernels for 12%

profile of v1, /device:TPU:0, one launch (start us, length us, event | category | flops | bytes accessed | tf_op | source)
XLA Modules:
  0.0 121.0 jit_solution(6121717756203600629)
XLA Ops:
  0.6 0.7 broadcast_in_dim.6
  1.4 0.1 mul.128
  1.5 1.9 %fusion.19 = f32[4096,64]{0,1:T(8,128)S(1)} fusion(f32[64]{0:T(128)} %constant.57.clone, s32[64]{0:T(128)S(1)} %mul.128), kind=kLoop, calls=%fused_computation.31 | loop fusion | flops 9699328 | bytes 1049088 | tf_op jit(solution)/shard_map/convert_element_type | solution.py:324
  3.4 3.7 %multiply_convert_fusion = bf16[4096,8,64]{0,2,1:T(8,128)(2,1)} fusion(f32[4096,64]{0,1:T(8,128)S(1)} %fusion.19, f32[4096,8]{0,1:T(8,128)} %constant.58.clone), kind=kLoop, calls=%fused_computation | loop fusion | flops 4194304 | bytes 5373952 | tf_op jit(solution)/shard_map/convert_element_type | solution.py:326
  7.1 0.0 copy-start.5
  7.1 6.5 %copy.11.w_ref = bf16[4096,512]{1,0:T(8,128)(2,1)} copy(bf16[4096,512]{0,1:T(8,128)(2,1)} %bitcast.15) | data formatting | bytes 8388608 | tf_op jit(solution)/shard_map/convert_element_type | solution.py:326
  13.5 0.0 copy-done.5
  13.5 0.7 broadcast_in_dim.16.mix_ref
  14.2 0.0 copy-start.6
  14.2 0.0 copy-start.1
  14.2 0.0 copy-start.2
  14.2 58.0 %spectra.1 = bf16[64,48,128]{2,1,0:T(8,128)(2,1)} custom-call(bf16[128,258048]{1,0:T(8,128)(2,1)} %bitcast.17, bf16[4096,512]{1,0:T(8,128)(2,1)} %copy.11.w_ref, f32[4,8,8,128]{3,2,1,0:T(8,128)} %broadcast_in_dim.16.mix_ref), custom_call_target="tpu_custom_call" | custom-call | flops 33822867456 | bytes 66060288 | tf_op jit(solution)/shard_map/spectra/pallas_call | solution.py:134
  72.2 7.3 %all-to-all-start = ((bf16[32,2,48,128]{3,2,1,0:T(8,128)(2,1)}), bf16[32,2,48,128]{3,2,1,0:T(8,128)(2,1)S(1)}, u32[]{:S(2)}, u32[]{:S(2)}) async-start(bf16[32,2,48,128]{3,2,1,0:T(8,128)(2,1)} %bitcast.16), calls=%async_computation | async-start | bytes 1572864 | tf_op jit(solution)/shard_map/all_to_all | solution.py:331
  79.5 0.0 copy-done.6
  79.5 0.6 dynamic_slice.4
  80.7 0.0 copy-done.1
  80.8 0.0 copy-done.2
  80.8 0.0 copy-start
  80.8 1.6 %copy-done = f32[512,1024]{1,0:T(8,128)S(1)} copy-done((f32[512,1024]{1,0:T(8,128)S(1)}, f32[512,1024]{1,0:T(8,128)}, u32[]{:S(2)}) %copy-start) | copy-done | bytes 2097176
  82.4 6.8 %steering.1 = (bf16[2,512,1024]{2,1,0:T(8,128)(2,1)S(1)}, bf16[1024,1024]{1,0:T(8,128)(2,1)S(1)}) custom-call(f32[1,1]{1,0:T(1,128)} %bitcast.4.bin_ref, f32[512,1024]{1,0:T(8,128)S(1)} %copy-done, s32[1,512]{1,0:T(1,128)S(1)} %bitcast.14, s32[1,1024]{1,0:T(1,128)S(1)} %bitcast.13), custom_call_target="tpu_custom_call" | custom-call | flops 3242196992 | bytes 4194304 | tf_op jit(solution)/shard_map/steering/pallas_call | solution.py:203
  89.1 0.0 copy-start.3
  89.1 1.3 %copy-done.3 = bf16[1024,1024]{1,0:T(8,128)(2,1)} copy-done((bf16[1024,1024]{1,0:T(8,128)(2,1)}, bf16[1024,1024]{1,0:T(8,128)(2,1)S(1)}, u32[]{:S(2)}) %copy-start.3) | copy-done | bytes 2097176
  90.5 11.0 %all-to-all-done = bf16[32,2,48,128]{3,2,1,0:T(8,128)(2,1)S(1)} async-done(((bf16[32,2,48,128]{3,2,1,0:T(8,128)(2,1)}), bf16[32,2,48,128]{3,2,1,0:T(8,128)(2,1)S(1)}, u32[]{:S(2)}, u32[]{:S(2)}) %all-to-all-start) | async-done | bytes 786464 | tf_op jit(solution)/shard_map/all_to_all | solution.py:331
  101.5 2.0 %beams.1 = bf16[8,64,384]{2,1,0:T(8,128)(2,1)} custom-call(bf16[4,8,2,48,128]{4,3,2,1,0:T(8,128)(2,1)S(1)} %bitcast.11, bf16[2,512,1024]{2,1,0:T(8,128)(2,1)S(1)} %get-tuple-element.5.table_ref), custom_call_target="tpu_custom_call" | custom-call | tf_op jit(solution)/shard_map/beams/pallas_call | solution.py:251
  103.5 3.6 %all-to-all-start.1 = ((bf16[8,64,384]{2,1,0:T(8,128)(2,1)}), bf16[8,64,384]{2,1,0:T(8,128)(2,1)S(1)}, u32[]{:S(2)}, u32[]{:S(2)}) async-start(bf16[8,64,384]{2,1,0:T(8,128)(2,1)} %beams.1), calls=%async_computation.1 | async-start | bytes 786432 | tf_op jit(solution)/shard_map/all_to_all | solution.py:340
  107.1 0.0 copy-start.4
  107.1 1.6 %copy-done.4 = bf16[1024,1024]{1,0:T(8,128)(2,1)S(1)} copy-done((bf16[1024,1024]{1,0:T(8,128)(2,1)S(1)}, bf16[1024,1024]{1,0:T(8,128)(2,1)}, u32[]{:S(2)}) %copy-start.4) | copy-done | bytes 2097176
  108.7 7.2 %visibilities.1 = f32[1,2,1024,1024]{3,2,1,0:T(8,128)} custom-call(bf16[4,8,2,48,128]{4,3,2,1,0:T(8,128)(2,1)S(1)} %bitcast.12, bf16[1024,1024]{1,0:T(8,128)(2,1)S(1)} %copy-done.4), custom_call_target="tpu_custom_call" | custom-call | flops 3221225472 | bytes 8388608 | tf_op jit(solution)/shard_map/visibilities/pallas_call | solution.py:283
  115.9 2.7 %all-to-all-done.1 = bf16[8,64,384]{2,1,0:T(8,128)(2,1)S(1)} async-done(((bf16[8,64,384]{2,1,0:T(8,128)(2,1)}), bf16[8,64,384]{2,1,0:T(8,128)(2,1)S(1)}, u32[]{:S(2)}, u32[]{:S(2)}) %all-to-all-start.1) | async-done | bytes 393248 | tf_op jit(solution)/shard_map/all_to_all | solution.py:340
  118.7 0.1 convert_bitcast_fusion
  118.7 0.8 reshape.108
  119.5 1.6 %copy.12 = f32[64,8,2,192]{3,2,1,0:T(2,128)} copy(f32[64,8,2,192]{3,2,0,1:T(2,128)S(1)} %reshape.108) | data formatting | bytes 1572864
Async XLA Ops:
  7.1 6.5 %copy-start.5 = (f32[4,8,128]{2,1,0:T(8,128)S(1)}, f32[4,8,128]{2,1,0:T(8,128)}, u32[]{:S(2)}) copy-start(f32[4,8,128]{2,1,0:T(8,128)} %constant.60) | copy-start | bytes 49156
  14.2 65.3 %copy-start.6 = (s32[32]{0:T(128)S(1)}, s32[32]{0:T(128)}, u32[]{:S(2)}) copy-start(s32[32]{0:T(128)} %param.9) | copy-start | bytes 388
  14.2 66.5 %copy-start.1 = (s32[1024]{0:T(1024)S(1)}, s32[1024]{0:T(1024)}, u32[]{:S(2)}) copy-start(s32[1024]{0:T(1024)} %param.10) | copy-start | bytes 12292
  14.2 66.5 %copy-start.2 = (s32[512]{0:T(512)S(1)}, s32[512]{0:T(512)}, u32[]{:S(2)}) copy-start(s32[512]{0:T(512)} %param.11) | copy-start | bytes 6148
  72.2 29.3 %all-to-all-start = ((bf16[32,2,48,128]{3,2,1,0:T(8,128)(2,1)}), bf16[32,2,48,128]{3,2,1,0:T(8,128)(2,1)S(1)}, u32[]{:S(2)}, u32[]{:S(2)}) async-start(bf16[32,2,48,128]{3,2,1,0:T(8,128)(2,1)} %bitcast.16), calls=%async_computation | async-start | bytes 1572864 | tf_op jit(solution)/shard_map/all_to_all | solution.py:331
  80.8 1.6 %copy-start = (f32[512,1024]{1,0:T(8,128)S(1)}, f32[512,1024]{1,0:T(8,128)}, u32[]{:S(2)}) copy-start(f32[512,1024]{1,0:T(8,128)} %delays_ref.1) | copy-start | bytes 6291460
  89.1 1.3 %copy-start.3 = (bf16[1024,1024]{1,0:T(8,128)(2,1)}, bf16[1024,1024]{1,0:T(8,128)(2,1)S(1)}, u32[]{:S(2)}) copy-start(bf16[1024,1024]{1,0:T(8,128)(2,1)S(1)} %get-tuple-element.4.place_ref) | copy-start | bytes 6291460
  103.5 15.2 %all-to-all-start.1 = ((bf16[8,64,384]{2,1,0:T(8,128)(2,1)}), bf16[8,64,384]{2,1,0:T(8,128)(2,1)S(1)}, u32[]{:S(2)}, u32[]{:S(2)}) async-start(bf16[8,64,384]{2,1,0:T(8,128)(2,1)} %beams.1), calls=%async_computation.1 | async-start | bytes 786432 | tf_op jit(solution)/shard_map/all_to_all | solution.py:340
  107.1 1.6 %copy-start.4 = (bf16[1024,1024]{1,0:T(8,128)(2,1)S(1)}, bf16[1024,1024]{1,0:T(8,128)(2,1)}, u32[]{:S(2)}) copy-start(bf16[1024,1024]{1,0:T(8,128)(2,1)} %copy-done.3) | copy-start | bytes 6291460

commit v2 on v1

--- a/solution.py
+++ b/solution.py
@@ -40,10 +40,11 @@
 
 def term_tiles(parity, per_tile):
     tiles = []
-    for wanted in (1.0, -1.0):
-        group = [r for r in range(RANK) if parity[r] == wanted]
-        for at in range(0, len(group), per_tile):
-            tiles.append((tuple(group[at : at + per_tile]), wanted))
+    for half in (range(RANK // 2), range(RANK // 2, RANK)):
+        for wanted in (1.0, -1.0):
+            group = [r for r in half if parity[r] == wanted]
+            for at in range(0, len(group), per_tile):
+                tiles.append((tuple(group[at : at + per_tile]), wanted))
     return tiles
 
 
@@ -57,94 +58,189 @@
     return angle + angle * square * total
 
 
-def spectra_kernel(chunk, chunks_per_step, frames, width, signs,
-                   x_ref, w_ref, mix_ref, out_ref, y_ref, acc_ref, turned_ref):
+def fill_weights(bins_ref, basis_ref, w_ref, width, out_tiles):
+    columns = w_ref.shape[1]
+    splits = basis_ref.shape[1]
+    block = 2 * LANES
+    half = NFFT // 2
+    source = lax.broadcasted_iota(jnp.int32, (splits, columns), 0)
+    term = lax.broadcasted_iota(jnp.int32, (splits, columns), 1) // width
+    spread = jnp.where(source % RANK == term, 1.0, 0.0).astype(jnp.bfloat16)
+    lane = lax.broadcasted_iota(jnp.int32, (1, LANES), 1)
+    quarter = jnp.where(lane % 2 == 1, 0.25, 0.0)
+    lane_bins = []
+    for out_tile in range(out_tiles):
+        channel = (lane + out_tile * LANES) % width // 2
+        value = jnp.zeros((1, LANES), jnp.int32)
+        for at in range(width // 2):
+            value = jnp.where(channel == at, bins_ref[at], value)
+        lane_bins.append(value)
+
+    def some(at, carry):
+        windows = [pl.ds(pl.multiple_of(at * block + i * half, block), block) for i in range(2)]
+        rows = lax.broadcasted_iota(jnp.int32, (block, LANES), 0) + at * block
+        factors = [
+            jnp.dot(basis_ref[window, :], spread, preferred_element_type=jnp.float32)
+            for window in windows
+        ]
+        for out_tile, bins in enumerate(lane_bins):
+            turns = rows.astype(jnp.float32) * (bins.astype(jnp.float32) * (1.0 / NFFT))
+            turns = turns - jnp.round(turns)
+            table = cos_turns(turns + quarter) * (1.0 / math.sqrt(NFFT))
+            table = table.astype(jnp.bfloat16).astype(jnp.float32)
+            flipped = table * jnp.where(bins % 2 == 1, -1.0, 1.0)
+            for tile in range(out_tile, columns // LANES, out_tiles):
+                lanes = slice(tile * LANES, (tile + 1) * LANES)
+                for window, values, factor in zip(windows, (table, flipped), factors):
+                    w_ref[window, lanes] = (values * factor[:, lanes]).astype(w_ref.dtype)
+        return carry
+
+    lax.fori_loop(0, half // block, some, 0)
+
+
+def spectra_kernel(chunk, frames, width, signs,
+                   bins_ref, basis_ref, mix_ref, minor_mix_ref, x_ref, out_ref,
+                   w_ref, major_ref, minor_ref, acc_ref, turned_ref):
     step = pl.program_id(0)
     signals = x_ref.shape[0]
     columns = w_ref.shape[1]
-    lag = (TAPS - 1 + chunk - 1) // chunk + 1
+    behind = TAPS - 1 + chunk
+    pad = behind % chunk
     size = min(width, LANES)
     out_tiles = width // size
-    per_tile = LANES // size
-
-    def combine(first, slot):
+
+    @pl.when(step == 0)
+    def _():
+        fill_weights(bins_ref, basis_ref, w_ref, width, out_tiles)
+        major_ref[: behind + pad] = jnp.zeros((behind + pad,) + major_ref.shape[1:], jnp.float32)
+        minor_ref[: behind + pad] = jnp.zeros((behind + pad,) + minor_ref.shape[1:], jnp.bfloat16)
+
+    def weigh(totals, held, factors, sign):
+        for k in range(TAPS // 2):
+            for o in range(chunk):
+                low, high = held[o + k], held[o + TAPS - 1 - k]
+                totals[o] = totals[o] + factors[k] * (low + high if sign > 0 else low - high)
+
+    def combine(slot, start):
+        first = jnp.maximum(slot * chunk - behind + pad, 0)
+        seen = None
         for out_tile in range(out_tiles):
-            for row in range(0, signals, 8):
-                totals = [jnp.zeros((8, LANES), jnp.float32) for _ in range(chunk)]
-                for tile in range(out_tile, columns // LANES, out_tiles):
-                    held = [
-                        y_ref[first + i, row : row + 8, tile * LANES : (tile + 1) * LANES]
-                        for i in range(chunk + TAPS - 1)
-                    ]
-                    for k in range(TAPS // 2):
-                        factor = mix_ref[tile, k]
-                        for o in range(chunk):
-                            low, high = held[o + k], held[o + TAPS - 1 - k]
-                            both = low + high if signs[tile // out_tiles] > 0 else low - high
-                            totals[o] = totals[o] + factor * both
+            small = [jnp.zeros((16, LANES), jnp.bfloat16) for _ in range(chunk)]
+            for tile in range(out_tile, columns // 2 // LANES, out_tiles):
+                lanes = slice(tile * LANES, (tile + 1) * LANES)
+                held = [minor_ref[first + i, pl.ds(start, 16), lanes] for i in range(chunk + TAPS - 1)]
+                factors = [minor_mix_ref[tile, k] for k in range(TAPS // 2)]
+                weigh(small, held, factors, signs[(columns // 2 // LANES + tile) // out_tiles])
+            wide = [total.astype(jnp.float32) for total in small]
+            for row in (0, 8):
+                window = pl.ds(start + row, 8)
+                totals = [total[row : row + 8] for total in wide]
+                for tile in range(out_tile, columns // 2 // LANES, out_tiles):
+                    lanes = slice(tile * LANES, (tile + 1) * LANES)
+                    held = [major_ref[first + i, window, lanes] for i in range(chunk + TAPS - 1)]
+                    factors = [mix_ref[tile, k : k + 1, :] for k in range(TAPS // 2)]
+                    weigh(totals, held, factors, signs[tile // out_tiles])
                 for o in range(chunk):
-                    acc_ref[o, row : row + 8, :] = totals[o]
-            for o in range(chunk):
-                turned = acc_ref[o].T
-                total = turned[:size]
-                for i in range(1, per_tile):
-                    total = total + turned[i * size : (i + 1) * size]
-                turned_ref[slot * chunk + o, out_tile * size : (out_tile + 1) * size, :] = total
-
-    def one_chunk(inner, carry):
-        at = step * chunks_per_step + inner
-        combine(jnp.maximum(at - lag, 0) * chunk, at)
-        rows = jnp.concatenate(
-            [
-                x_ref[:, pl.ds(pl.multiple_of((inner * chunk + i) * NFFT, NFFT), NFFT)]
-                for i in range(chunk)
-            ],
-            axis=0,
+                    acc_ref[slot * chunk + o, out_tile, window, :] = totals[o]
+                    seen = totals[o] if seen is None else seen + totals[o]
+        return jnp.maximum(jnp.minimum(seen, 0.0), 0.0)
+
+    def turn(slot):
+        unit = jnp.where(
+            lax.broadcasted_iota(jnp.int32, (size, 2 * LANES), 0)
+            == lax.broadcasted_iota(jnp.int32, (size, 2 * LANES), 1) % size, 1.0, 0.0
+        ).astype(jnp.bfloat16)
+        together = chunk if signals % LANES == 0 else 1
+        for out_tile in range(out_tiles):
+            for at in range(0, chunk, together):
+                total = jnp.concatenate(
+                    [acc_ref[slot * chunk + at + i, out_tile] for i in range(together)], axis=0
+                )
+                high = total.astype(jnp.bfloat16)
+                low = (total - high.astype(jnp.float32)).astype(jnp.bfloat16)
+                both = jnp.concatenate([high, low], axis=1)
+                turned = lax.dot_general(unit, both, NT, preferred_element_type=jnp.float32)
+                for i in range(together):
+                    turned_ref[out_tile * size : (out_tile + 1) * size, slot * chunk + at + i, :] = (
+                        turned[:, i * signals : (i + 1) * signals]
+                    )
+
+    turn(jnp.maximum(step - 1, 0))
+    pieces = 16
+    depth = NFFT // pieces
+    zero = product = None
+    for piece in range(pieces):
+        parts = [x_ref[:, i * NFFT + piece * depth : i * NFFT + (piece + 1) * depth] for i in range(chunk)]
+        if zero is not None:
+            zero = jnp.concatenate([zero, zero], axis=0).astype(jnp.bfloat16)
+            top = jnp.concatenate([parts[0][:16, :LANES] + zero, parts[0][:16, LANES:]], axis=1)
+            parts[0] = jnp.concatenate([top, parts[0][16:]], axis=0)
+        part = jnp.dot(
+            jnp.concatenate(parts, axis=0),
+            w_ref[piece * depth : (piece + 1) * depth, :],
+            preferred_element_type=jnp.float32,
         )
-        product = jnp.dot(rows, w_ref[...], preferred_element_type=jnp.float32)
-        y_ref[pl.ds(at * chunk, chunk)] = product.reshape(chunk, signals, columns)
-        return carry
-
-    lax.fori_loop(0, chunks_per_step, one_chunk, 0)
+        product = part if product is None else product + part
+        zero = None
+        for start in range(piece * 16, signals, pieces * 16):
+            zero = combine(step, start)
+    window = pl.ds(step * chunk + pad, chunk)
+    major_ref[window] = product[:, : columns // 2].reshape(chunk, signals, columns // 2)
+    minor = product[:, columns // 2 :].astype(jnp.bfloat16)
+    minor_ref[window] = minor.reshape(chunk, signals, columns // 2)
 
     @pl.when(step == pl.num_programs(0) - 1)
     def _():
         chunks = (frames + TAPS - 1) // chunk
-
-        def rest(group, carry):
-            combine(group * chunk, group + lag)
-            return carry
-
-        lax.fori_loop(chunks - lag, frames // chunk, rest, 0)
+        for start in range(0, signals, 16):
+            combine(chunks, start)
+        turn(chunks - 1)
+        turn(chunks)
         for row in range(width):
-            out_ref[row] = turned_ref[pl.ds(lag * chunk, frames), row, :].astype(out_ref.dtype)
-
-
-def spectra_of(samples, weights, mix, signs, frames):
+            out_ref[row] = turned_ref[row, behind : behind + frames, :].astype(out_ref.dtype)
+
+
+def spectra_of(samples, chan_bins, frames):
     signals, length = samples.shape
     in_frames = length // NFFT
-    columns = weights.shape[1]
-    width = columns // RANK
-    chunk = math.gcd(3, math.gcd(in_frames, frames))
-    chunks = in_frames // chunk
-    per_step = next(d for d in (3, 2, 1) if chunks % d == 0)
-    lag = (TAPS - 1 + chunk - 1) // chunk + 1
-    body = functools.partial(spectra_kernel, chunk, per_step, frames, width, signs)
-    block = per_step * chunk * NFFT
+    width = 2 * chan_bins.shape[0]
+    columns = RANK * width
+    size = min(width, LANES)
+    out_tiles = width // size
+    chunk = max(d for d in (1, 2, 3) if in_frames % d == 0)
+    behind = TAPS - 1 + chunk
+    slots = (in_frames // chunk + 1) * chunk
+
+    mix, basis, parity = taps_factors()
+    tiles = term_tiles(parity, LANES // size)
+    signs = tuple(sign for _, sign in tiles)
+    order = [r for terms, _ in tiles for r in terms]
+    lanes = np.repeat(mix[: TAPS // 2, order], width, axis=1).astype(np.float32)
+    lanes = lanes.reshape(TAPS // 2, -1, LANES).transpose(1, 0, 2)
+    major, minor = np.split(lanes, 2)
+    minor = np.repeat(minor[:, :, None, :], 16, axis=2).astype(jnp.bfloat16)
+    pieces, left = [], basis[order].T.astype(np.float32)
+    for _ in range(3):
+        pieces.append(left.astype(jnp.bfloat16))
+        left = left - pieces[-1].astype(np.float32)
+    pieces.append(np.zeros((NFFT, LANES - 3 * RANK), jnp.bfloat16))
+
+    whole = pl.BlockSpec(memory_space=pltpu.VMEM)
     return pl.pallas_call(
-        body,
-        grid=(chunks // per_step,),
+        functools.partial(spectra_kernel, chunk, frames, width, signs),
+        grid=(in_frames // chunk,),
         in_specs=[
-            pl.BlockSpec((signals, block), lambda i: (0, i)),
-            pl.BlockSpec(weights.shape, lambda i: (0, 0), pipeline_mode=pl.Buffered(1)),
-            pl.BlockSpec(mix.shape, lambda i: (0, 0, 0, 0), pipeline_mode=pl.Buffered(1)),
+            pl.BlockSpec(memory_space=pltpu.SMEM), whole, whole, whole,
+            pl.BlockSpec((signals, chunk * NFFT), lambda i: (0, i)),
         ],
         out_specs=pl.BlockSpec((width, frames, signals), lambda i: (0, 0, 0)),
         out_shape=jax.ShapeDtypeStruct((width, frames, signals), jnp.bfloat16),
         scratch_shapes=[
-            pltpu.VMEM((in_frames, signals, columns), jnp.float32),
-            pltpu.VMEM((chunk, signals, LANES), jnp.float32),
-            pltpu.VMEM((frames + lag * chunk, width, signals), jnp.float32),
+            pltpu.VMEM((NFFT, columns), jnp.bfloat16),
+            pltpu.VMEM((in_frames + behind % chunk, signals, columns // 2), jnp.float32),
+            pltpu.VMEM((in_frames + behind % chunk, signals, columns // 2), jnp.bfloat16),
+            pltpu.VMEM((slots, out_tiles, signals, LANES), jnp.float32),
+            pltpu.VMEM((width, slots, signals), jnp.float32),
         ],
         compiler_params=pltpu.CompilerParams(vmem_limit_bytes=60 << 20),
         cost_estimate=pl.CostEstimate(
@@ -153,7 +249,7 @@
             transcendentals=0,
         ),
         name="spectra",
-    )(samples, weights, mix)
+    )(chan_bins, jnp.asarray(np.concatenate(pieces, axis=1)), jnp.asarray(major), jnp.asarray(minor), samples)
 
 
 def steering_kernel(bin_ref, delays_ref, beams_ref, antennas_ref, table_ref, place_ref, raw_ref):
@@ -308,25 +404,7 @@
     freq_count = lax.axis_size("freq")
     times = tm_count * frames
 
-    mix, basis, parity = taps_factors()
-    per_tile = max(1, LANES // (2 * channels))
-    tiles = term_tiles(parity, per_tile)
-    order = [r for terms, _ in tiles for r in terms]
-    signs = tuple(sign for _, sign in tiles)
-    lanes = np.repeat(mix[: TAPS // 2, order], 2 * channels, axis=1).astype(np.float32)
-    lanes = lanes.reshape(TAPS // 2, -1, 1, LANES).transpose(1, 0, 2, 3)
-    mix_lanes = jnp.broadcast_to(jnp.asarray(lanes), (lanes.shape[0], TAPS // 2, 8, LANES))
-
-    positions = jnp.arange(NFFT, dtype=jnp.int32)
-    products = positions[:, None] * jnp.repeat(chan_bins, 2)[None, :] % NFFT
-    quarter = jnp.asarray(np.tile(np.array([0.0, 0.25], np.float32), channels))
-    table = cos_turns(products.astype(jnp.float32) * (1.0 / NFFT) + quarter)
-    table = (table * (1.0 / math.sqrt(NFFT))).astype(jnp.bfloat16).astype(jnp.float32)
-    basis_columns = jnp.asarray(basis[order].T.astype(np.float32))
-    weights = (basis_columns[:, :, None] * table[:, None, :]).astype(jnp.bfloat16)
-    weights = weights.reshape(NFFT, RANK * 2 * channels)
-
-    spectra = spectra_of(voltages[0], weights, mix_lanes, signs, frames)
+    spectra = spectra_of(voltages[0], chan_bins, frames)
     spectra = spectra.reshape(channels, 2, frames, signals_dev)
     moved = lax.all_to_all(spectra, ("tm", "freq"), split_axis=0, concat_axis=0, tiled=True)
     moved = moved.reshape(tm_count, freq_count, 2, frames, signals_dev)

time: 122 us -> 98.5 us (0.81)
  Pallas kernels: 74 us -> 64.3 us
  local copies, waits for them, and re-layouts: 15.4 us -> 7.4 us
  other arithmetic: 5.65 us -> 0.06 us
    pallas_call x1, Pallas kernels: 58 us -> 48.3 us  [spectra_of(): pl.pallas_call(functools.partial(spectra_kernel, chunk, frames, width, si...]
    convert_element_type x1 -> x0, local copies, waits for them, and re-layouts: 6.48 us -> none  [body(): (basis_columns[:, :, None] * table[:, None, :]).astype(jnp.bfloat16)]
    convert_element_type x2 -> x0, other arithmetic: 5.59 us -> none  [the longest x1 3.67 us: body(): (basis_columns[:, :, None] * table[:, None, :]).astype(jnp.bfloat16)]
    broadcast_in_dim x2 -> x0, local copies, waits for them, and re-layouts: 1.39 us -> none  [the longest x1 0.73 us: body(): products = positions[:, None] * jnp.repeat(chan_bins, 2)[None, :] % NFFT]
    unnamed x15 -> x13, local copies, waits for them, and re-layouts: 6.06 us -> 6.06 us
  transfers between devices with their start and end apart: 2 -> 2, of which waited for: 2 -> 2; matrix products, arithmetic and copies ran while one was open for 0% -> 1% of each run, Pallas kernels for 12% -> 14%
where the time goes in v2:
time: 98.5 us; the launch traced here: 97.9 us
  Pallas kernels  64.3 us (65%)
  waiting for transfers between devices  13.9 us (14%)
  starting transfers between devices  10.8 us (11%)
  local copies, waits for them, and re-layouts  7.4 us (8%)
  between operations  1.4 us (1%)
    pallas_call x1, Pallas kernels, spectra_of(): pl.pallas_call(functools.partial(spectra_kernel, chunk, frames, width, si...  48.3 us
    all_to_all x1, waiting for transfers between devices, body(): lax.all_to_all(spectra, ('tm', 'freq'), split_axis=0, concat_axis=0, tile...  11 us
    all_to_all x1, starting transfers between devices, body(): lax.all_to_all(spectra, ('tm', 'freq'), split_axis=0, concat_axis=0, tile...  7.3 us
    pallas_call x1, Pallas kernels, visibilities_of(): pl.pallas_call(visibility_kernel, grid=(antennas // rows,), in_specs=[pl....  7.21 us
    pallas_call x1, Pallas kernels, steering_of(): pl.pallas_call(steering_kernel, in_specs=[pl.BlockSpec(memory_space=pltpu...  6.77 us
    unnamed x13, local copies, waits for them, and re-layouts  6.06 us
    all_to_all x1, starting transfers between devices, body(): lax.all_to_all(formed, 'freq', split_axis=0, concat_axis=0, tiled=True)  3.45 us
    all_to_all x1, waiting for transfers between devices, body(): lax.all_to_all(formed, 'freq', split_axis=0, concat_axis=0, tiled=True)  2.92 us
  transfers between devices with their start and end apart: 2, of which 2 were waited for; matrix products, arithmetic and copies ran while one was open for 1% of the time, Pallas kernels for 14%

profile of v2, /device:TPU:0, one launch (start us, length us, event | category | flops | bytes accessed | tf_op | source)
XLA Modules:
  0.0 97.9 jit_solution(8356588281761681903)
XLA Ops:
  0.6 0.0 copy-start.5
  0.6 0.0 copy-start.1
  0.7 0.0 copy-start.2
  0.7 48.3 %spectra.1 = bf16[64,48,128]{2,1,0:T(8,128)(2,1)} custom-call(s32[32]{0:T(128)} %bins_ref.1, bf16[4096,128]{1,0:T(8,128)(2,1)} %constant.22.clone.basis_ref, f32[2,8,128]{2,1,0:T(8,128)} %constant.23.clone.mix_ref, bf16[2,8,16,128]{3,2,1,0:T(8,128)(2,1)} %constant.24.clone.minor_mix_ref, bf16[128,258048]{1,0:T(8,128)(2,1)} %bitcast.15), custom_call_target="tpu_custom_call" | custom-call | flops 33822867456 | bytes 66060288 | tf_op jit(solution)/shard_map/spectra/pallas_call | solution.py:229
  49.0 7.3 %all-to-all-start = ((bf16[32,2,48,128]{3,2,1,0:T(8,128)(2,1)}), bf16[32,2,48,128]{3,2,1,0:T(8,128)(2,1)S(1)}, u32[]{:S(2)}, u32[]{:S(2)}) async-start(bf16[32,2,48,128]{3,2,1,0:T(8,128)(2,1)} %bitcast.14), calls=%async_computation | async-start | bytes 1572864 | tf_op jit(solution)/shard_map/all_to_all | solution.py:409
  56.3 0.0 copy-done.5
  56.3 0.6 dynamic_slice.4
  57.6 0.0 copy-done.1
  57.6 0.0 copy-done.2
  57.6 0.0 copy-start
  57.6 1.6 %copy-done = f32[512,1024]{1,0:T(8,128)S(1)} copy-done((f32[512,1024]{1,0:T(8,128)S(1)}, f32[512,1024]{1,0:T(8,128)}, u32[]{:S(2)}) %copy-start) | copy-done | bytes 2097176
  59.2 6.8 %steering.1 = (bf16[2,512,1024]{2,1,0:T(8,128)(2,1)S(1)}, bf16[1024,1024]{1,0:T(8,128)(2,1)S(1)}) custom-call(f32[1,1]{1,0:T(1,128)} %bitcast.3.bin_ref, f32[512,1024]{1,0:T(8,128)S(1)} %copy-done, s32[1,512]{1,0:T(1,128)S(1)} %bitcast.13, s32[1,1024]{1,0:T(1,128)S(1)} %bitcast.12), custom_call_target="tpu_custom_call" | custom-call | flops 3242196992 | bytes 4194304 | tf_op jit(solution)/shard_map/steering/pallas_call | solution.py:299
  66.0 0.0 copy-start.3
  66.0 1.3 %copy-done.3 = bf16[1024,1024]{1,0:T(8,128)(2,1)} copy-done((bf16[1024,1024]{1,0:T(8,128)(2,1)}, bf16[1024,1024]{1,0:T(8,128)(2,1)S(1)}, u32[]{:S(2)}) %copy-start.3) | copy-done | bytes 2097176
  67.3 11.0 %all-to-all-done = bf16[32,2,48,128]{3,2,1,0:T(8,128)(2,1)S(1)} async-done(((bf16[32,2,48,128]{3,2,1,0:T(8,128)(2,1)}), bf16[32,2,48,128]{3,2,1,0:T(8,128)(2,1)S(1)}, u32[]{:S(2)}, u32[]{:S(2)}) %all-to-all-start) | async-done | bytes 786464 | tf_op jit(solution)/shard_map/all_to_all | solution.py:409
  78.3 2.0 %beams.1 = bf16[8,64,384]{2,1,0:T(8,128)(2,1)} custom-call(bf16[4,8,2,48,128]{4,3,2,1,0:T(8,128)(2,1)S(1)} %bitcast.10, bf16[2,512,1024]{2,1,0:T(8,128)(2,1)S(1)} %get-tuple-element.5.table_ref), custom_call_target="tpu_custom_call" | custom-call | tf_op jit(solution)/shard_map/beams/pallas_call | solution.py:347
  80.3 3.5 %all-to-all-start.1 = ((bf16[8,64,384]{2,1,0:T(8,128)(2,1)}), bf16[8,64,384]{2,1,0:T(8,128)(2,1)S(1)}, u32[]{:S(2)}, u32[]{:S(2)}) async-start(bf16[8,64,384]{2,1,0:T(8,128)(2,1)} %beams.1), calls=%async_computation.1 | async-start | bytes 786432 | tf_op jit(solution)/shard_map/all_to_all | solution.py:418
  83.8 0.0 copy-start.4
  83.8 1.6 %copy-done.4 = bf16[1024,1024]{1,0:T(8,128)(2,1)S(1)} copy-done((bf16[1024,1024]{1,0:T(8,128)(2,1)S(1)}, bf16[1024,1024]{1,0:T(8,128)(2,1)}, u32[]{:S(2)}) %copy-start.4) | copy-done | bytes 2097176
  85.4 7.2 %visibilities.1 = f32[1,2,1024,1024]{3,2,1,0:T(8,128)} custom-call(bf16[4,8,2,48,128]{4,3,2,1,0:T(8,128)(2,1)S(1)} %bitcast.11, bf16[1024,1024]{1,0:T(8,128)(2,1)S(1)} %copy-done.4), custom_call_target="tpu_custom_call" | custom-call | flops 3221225472 | bytes 8388608 | tf_op jit(solution)/shard_map/visibilities/pallas_call | solution.py:379
  92.6 2.9 %all-to-all-done.1 = bf16[8,64,384]{2,1,0:T(8,128)(2,1)S(1)} async-done(((bf16[8,64,384]{2,1,0:T(8,128)(2,1)}), bf16[8,64,384]{2,1,0:T(8,128)(2,1)S(1)}, u32[]{:S(2)}, u32[]{:S(2)}) %all-to-all-start.1) | async-done | bytes 393248 | tf_op jit(solution)/shard_map/all_to_all | solution.py:418
  95.5 0.1 convert_bitcast_fusion
  95.5 0.8 reshape.35
  96.3 1.6 %copy.10 = f32[64,8,2,192]{3,2,1,0:T(2,128)} copy(f32[64,8,2,192]{3,2,0,1:T(2,128)S(1)} %reshape.35) | data formatting | bytes 1572864
Async XLA Ops:
  0.6 55.7 %copy-start.5 = (s32[32]{0:T(128)S(1)}, s32[32]{0:T(128)}, u32[]{:S(2)}) copy-start(s32[32]{0:T(128)} %bins_ref.1) | copy-start | bytes 388
  0.6 56.9 %copy-start.1 = (s32[1024]{0:T(1024)S(1)}, s32[1024]{0:T(1024)}, u32[]{:S(2)}) copy-start(s32[1024]{0:T(1024)} %param.10) | copy-start | bytes 12292
  0.7 56.9 %copy-start.2 = (s32[512]{0:T(512)S(1)}, s32[512]{0:T(512)}, u32[]{:S(2)}) copy-start(s32[512]{0:T(512)} %param.11) | copy-start | bytes 6148
  49.0 29.3 %all-to-all-start = ((bf16[32,2,48,128]{3,2,1,0:T(8,128)(2,1)}), bf16[32,2,48,128]{3,2,1,0:T(8,128)(2,1)S(1)}, u32[]{:S(2)}, u32[]{:S(2)}) async-start(bf16[32,2,48,128]{3,2,1,0:T(8,128)(2,1)} %bitcast.14), calls=%async_computation | async-start | bytes 1572864 | tf_op jit(solution)/shard_map/all_to_all | solution.py:409
  57.6 1.6 %copy-start = (f32[512,1024]{1,0:T(8,128)S(1)}, f32[512,1024]{1,0:T(8,128)}, u32[]{:S(2)}) copy-start(f32[512,1024]{1,0:T(8,128)} %delays_ref.1) | copy-start | bytes 6291460
  66.0 1.3 %copy-start.3 = (bf16[1024,1024]{1,0:T(8,128)(2,1)}, bf16[1024,1024]{1,0:T(8,128)(2,1)S(1)}, u32[]{:S(2)}) copy-start(bf16[1024,1024]{1,0:T(8,128)(2,1)S(1)} %get-tuple-element.4.place_ref) | copy-start | bytes 6291460
  80.3 15.2 %all-to-all-start.1 = ((bf16[8,64,384]{2,1,0:T(8,128)(2,1)}), bf16[8,64,384]{2,1,0:T(8,128)(2,1)S(1)}, u32[]{:S(2)}, u32[]{:S(2)}) async-start(bf16[8,64,384]{2,1,0:T(8,128)(2,1)} %beams.1), calls=%async_computation.1 | async-start | bytes 786432 | tf_op jit(solution)/shard_map/all_to_all | solution.py:418
  83.8 1.6 %copy-start.4 = (bf16[1024,1024]{1,0:T(8,128)(2,1)S(1)}, bf16[1024,1024]{1,0:T(8,128)(2,1)}, u32[]{:S(2)}) copy-start(bf16[1024,1024]{1,0:T(8,128)(2,1)} %copy-done.3) | copy-start | bytes 6291460

commit v3 on v2

--- a/solution.py
+++ b/solution.py
@@ -99,16 +99,33 @@
 
 
 def spectra_kernel(chunk, frames, width, signs,
-                   bins_ref, basis_ref, mix_ref, minor_mix_ref, x_ref, out_ref,
-                   w_ref, major_ref, minor_ref, acc_ref, turned_ref):
+                   bins_ref, basis_ref, mix_ref, minor_mix_ref, samples_ref, out_ref,
+                   x_ref, arrived, w_ref, major_ref, minor_ref, acc_ref, turned_ref):
     step = pl.program_id(0)
-    signals = x_ref.shape[0]
+    steps = pl.num_programs(0)
+    signals = samples_ref.shape[0]
     columns = w_ref.shape[1]
     behind = TAPS - 1 + chunk
     pad = behind % chunk
     size = min(width, LANES)
     out_tiles = width // size
 
+    def fetch(at):
+        block = x_ref.shape[2]
+        return pltpu.make_async_copy(
+            samples_ref.at[:, pl.ds(pl.multiple_of(at * block, block), block)],
+            x_ref.at[at % 2],
+            arrived.at[at % 2],
+        )
+
+    @pl.when(step == 0)
+    def _():
+        fetch(0).start()
+
+    @pl.when(step + 1 < steps)
+    def _():
+        fetch(step + 1).start()
+
     @pl.when(step == 0)
     def _():
         fill_weights(bins_ref, basis_ref, w_ref, width, out_tiles)
@@ -117,18 +134,19 @@
 
     def weigh(totals, held, factors, sign):
         for k in range(TAPS // 2):
-            for o in range(chunk):
+            for o in range(len(totals)):
                 low, high = held[o + k], held[o + TAPS - 1 - k]
                 totals[o] = totals[o] + factors[k] * (low + high if sign > 0 else low - high)
 
-    def combine(slot, start):
-        first = jnp.maximum(slot * chunk - behind + pad, 0)
+    def combine(slot, begin, count, start):
+        first = jnp.maximum(slot * chunk - behind + pad, 0) + begin
+        frames_in = count + TAPS - 1
         seen = None
         for out_tile in range(out_tiles):
-            small = [jnp.zeros((16, LANES), jnp.bfloat16) for _ in range(chunk)]
+            small = [jnp.zeros((16, LANES), jnp.bfloat16) for _ in range(count)]
             for tile in range(out_tile, columns // 2 // LANES, out_tiles):
                 lanes = slice(tile * LANES, (tile + 1) * LANES)
-                held = [minor_ref[first + i, pl.ds(start, 16), lanes] for i in range(chunk + TAPS - 1)]
+                held = [minor_ref[first + i, pl.ds(start, 16), lanes] for i in range(frames_in)]
                 factors = [minor_mix_ref[tile, k] for k in range(TAPS // 2)]
                 weigh(small, held, factors, signs[(columns // 2 // LANES + tile) // out_tiles])
             wide = [total.astype(jnp.float32) for total in small]
@@ -137,13 +155,21 @@
                 totals = [total[row : row + 8] for total in wide]
                 for tile in range(out_tile, columns // 2 // LANES, out_tiles):
                     lanes = slice(tile * LANES, (tile + 1) * LANES)
-                    held = [major_ref[first + i, window, lanes] for i in range(chunk + TAPS - 1)]
+                    held = [major_ref[first + i, window, lanes] for i in range(frames_in)]
                     factors = [mix_ref[tile, k : k + 1, :] for k in range(TAPS // 2)]
                     weigh(totals, held, factors, signs[tile // out_tiles])
-                for o in range(chunk):
-                    acc_ref[slot * chunk + o, out_tile, window, :] = totals[o]
+                for o in range(count):
+                    acc_ref[slot * chunk + begin + o, out_tile, window, :] = totals[o]
                     seen = totals[o] if seen is None else seen + totals[o]
         return jnp.maximum(jnp.minimum(seen, 0.0), 0.0)
+
+    groups = -(-chunk // 4)
+    bounds = [chunk * i // groups for i in range(groups + 1)]
+    shares = [
+        (begin, end - begin, start)
+        for begin, end in zip(bounds[:-1], bounds[1:])
+        for start in range(0, signals, 16)
+    ]
 
     def turn(slot):
         unit = jnp.where(
@@ -165,35 +191,43 @@
                         turned[:, i * signals : (i + 1) * signals]
                     )
 
-    turn(jnp.maximum(step - 1, 0))
+    fetch(step).wait()
+    slot = step % 2
     pieces = 16
     depth = NFFT // pieces
-    zero = product = None
+    zero = None
+    turn(jnp.maximum(step - 1, 0))
+    product = None
     for piece in range(pieces):
-        parts = [x_ref[:, i * NFFT + piece * depth : i * NFFT + (piece + 1) * depth] for i in range(chunk)]
-        if zero is not None:
+        parts = [
+            x_ref[slot, :, i * NFFT + piece * depth : i * NFFT + (piece + 1) * depth]
+            for i in range(chunk)
+        ]
+        if zero is not None and any(share * pieces // len(shares) == piece for share in range(len(shares))):
             zero = jnp.concatenate([zero, zero], axis=0).astype(jnp.bfloat16)
             top = jnp.concatenate([parts[0][:16, :LANES] + zero, parts[0][:16, LANES:]], axis=1)
             parts[0] = jnp.concatenate([top, parts[0][16:]], axis=0)
+            zero = None
         part = jnp.dot(
             jnp.concatenate(parts, axis=0),
             w_ref[piece * depth : (piece + 1) * depth, :],
             preferred_element_type=jnp.float32,
         )
         product = part if product is None else product + part
-        zero = None
-        for start in range(piece * 16, signals, pieces * 16):
-            zero = combine(step, start)
+        for share in range(len(shares)):
+            if share * pieces // len(shares) == piece:
+                more = combine(step, *shares[share])
+                zero = more if zero is None else zero + more
     window = pl.ds(step * chunk + pad, chunk)
     major_ref[window] = product[:, : columns // 2].reshape(chunk, signals, columns // 2)
     minor = product[:, columns // 2 :].astype(jnp.bfloat16)
     minor_ref[window] = minor.reshape(chunk, signals, columns // 2)
 
-    @pl.when(step == pl.num_programs(0) - 1)
+    @pl.when(step == steps - 1)
     def _():
         chunks = (frames + TAPS - 1) // chunk
-        for start in range(0, signals, 16):
-            combine(chunks, start)
+        for share in shares:
+            combine(chunks, *share)
         turn(chunks - 1)
         turn(chunks)
         for row in range(width):
@@ -207,7 +241,7 @@
     columns = RANK * width
     size = min(width, LANES)
     out_tiles = width // size
-    chunk = max(d for d in (1, 2, 3) if in_frames % d == 0)
+    chunk = max(d for d in (1, 3, 7) if in_frames % d == 0)
     behind = TAPS - 1 + chunk
     slots = (in_frames // chunk + 1) * chunk
 
@@ -231,11 +265,13 @@
         grid=(in_frames // chunk,),
         in_specs=[
             pl.BlockSpec(memory_space=pltpu.SMEM), whole, whole, whole,
-            pl.BlockSpec((signals, chunk * NFFT), lambda i: (0, i)),
+            pl.BlockSpec(memory_space=pl.ANY),
         ],
         out_specs=pl.BlockSpec((width, frames, signals), lambda i: (0, 0, 0)),
         out_shape=jax.ShapeDtypeStruct((width, frames, signals), jnp.bfloat16),
         scratch_shapes=[
+            pltpu.VMEM((2, signals, chunk * NFFT), jnp.bfloat16),
+            pltpu.SemaphoreType.DMA((2,)),
             pltpu.VMEM((NFFT, columns), jnp.bfloat16),
             pltpu.VMEM((in_frames + behind % chunk, signals, columns // 2), jnp.float32),
             pltpu.VMEM((in_frames + behind % chunk, signals, columns // 2), jnp.bfloat16),

time: 98.5 us -> 96.1 us (0.976)
  Pallas kernels: 64.3 us -> 62.2 us
    pallas_call x1, Pallas kernels: 48.3 us -> 46.2 us  [spectra_of(): pl.pallas_call(functools.partial(spectra_kernel, chunk, frames, width, si...]
  transfers between devices with their start and end apart: 2 -> 2, of which waited for: 2 -> 2; matrix products, arithmetic and copies ran while one was open for 1% -> 1% of each run, Pallas kernels for 14% -> 15%
where the time goes in v3:
time: 96.1 us; the launch traced here: 95.7 us
  Pallas kernels  62.2 us (65%)
  waiting for transfers between devices  13.7 us (14%)
  starting transfers between devices  10.9 us (11%)
  local copies, waits for them, and re-layouts  7.4 us (8%)
  between operations  1.41 us (1%)
    pallas_call x1, Pallas kernels, spectra_of(): pl.pallas_call(functools.partial(spectra_kernel, chunk, frames, width, si...  46.2 us
    all_to_all x1, waiting for transfers between devices, body(): lax.all_to_all(spectra, ('tm', 'freq'), split_axis=0, concat_axis=0, tile...  11 us
    all_to_all x1, starting transfers between devices, body(): lax.all_to_all(spectra, ('tm', 'freq'), split_axis=0, concat_axis=0, tile...  7.3 us
    pallas_call x1, Pallas kernels, visibilities_of(): pl.pallas_call(visibility_kernel, grid=(antennas // rows,), in_specs=[pl....  7.21 us
    pallas_call x1, Pallas kernels, steering_of(): pl.pallas_call(steering_kernel, in_specs=[pl.BlockSpec(memory_space=pltpu...  6.76 us
    unnamed x13, local copies, waits for them, and re-layouts  6.06 us
    all_to_all x1, starting transfers between devices, body(): lax.all_to_all(formed, 'freq', split_axis=0, concat_axis=0, tiled=True)  3.63 us
    all_to_all x1, waiting for transfers between devices, body(): lax.all_to_all(formed, 'freq', split_axis=0, concat_axis=0, tiled=True)  2.73 us
  transfers between devices with their start and end apart: 2, of which 2 were waited for; matrix products, arithmetic and copies ran while one was open for 1% of the time, Pallas kernels for 15%

profile of v3, /device:TPU:0, one launch (start us, length us, event | category | flops | bytes accessed | tf_op | source)
XLA Modules:
  0.0 95.7 jit_solution(14083624961709085675)
XLA Ops:
  0.6 0.0 copy-start.5
  0.6 0.0 copy-start.1
  0.7 0.0 copy-start.2
  0.7 46.2 %spectra.1 = bf16[64,48,128]{2,1,0:T(8,128)(2,1)} custom-call(s32[32]{0:T(128)} %bins_ref.1, bf16[4096,128]{1,0:T(8,128)(2,1)} %constant.22.clone.basis_ref, f32[2,8,128]{2,1,0:T(8,128)} %constant.23.clone.mix_ref, bf16[2,8,16,128]{3,2,1,0:T(8,128)(2,1)} %constant.24.clone.minor_mix_ref, bf16[128,258048]{1,0:T(8,128)(2,1)} %bitcast.15), custom_call_target="tpu_custom_call" | custom-call | flops 33822867456 | bytes 66060288 | tf_op jit(solution)/shard_map/spectra/pallas_call | solution.py:263
  46.8 7.3 %all-to-all-start = ((bf16[32,2,48,128]{3,2,1,0:T(8,128)(2,1)}), bf16[32,2,48,128]{3,2,1,0:T(8,128)(2,1)S(1)}, u32[]{:S(2)}, u32[]{:S(2)}) async-start(bf16[32,2,48,128]{3,2,1,0:T(8,128)(2,1)} %bitcast.14), calls=%async_computation | async-start | bytes 1572864 | tf_op jit(solution)/shard_map/all_to_all | solution.py:445
  54.2 0.0 copy-done.5
  54.2 0.6 dynamic_slice.4
  55.4 0.0 copy-done.1
  55.4 0.0 copy-done.2
  55.4 0.0 copy-start
  55.4 1.6 %copy-done = f32[512,1024]{1,0:T(8,128)S(1)} copy-done((f32[512,1024]{1,0:T(8,128)S(1)}, f32[512,1024]{1,0:T(8,128)}, u32[]{:S(2)}) %copy-start) | copy-done | bytes 2097176
  57.0 6.8 %steering.1 = (bf16[2,512,1024]{2,1,0:T(8,128)(2,1)S(1)}, bf16[1024,1024]{1,0:T(8,128)(2,1)S(1)}) custom-call(f32[1,1]{1,0:T(1,128)} %bitcast.3.bin_ref, f32[512,1024]{1,0:T(8,128)S(1)} %copy-done, s32[1,512]{1,0:T(1,128)S(1)} %bitcast.13, s32[1,1024]{1,0:T(1,128)S(1)} %bitcast.12), custom_call_target="tpu_custom_call" | custom-call | flops 3242196992 | bytes 4194304 | tf_op jit(solution)/shard_map/steering/pallas_call | solution.py:335
  63.8 0.0 copy-start.3
  63.8 1.3 %copy-done.3 = bf16[1024,1024]{1,0:T(8,128)(2,1)} copy-done((bf16[1024,1024]{1,0:T(8,128)(2,1)}, bf16[1024,1024]{1,0:T(8,128)(2,1)S(1)}, u32[]{:S(2)}) %copy-start.3) | copy-done | bytes 2097176
  65.1 11.0 %all-to-all-done = bf16[32,2,48,128]{3,2,1,0:T(8,128)(2,1)S(1)} async-done(((bf16[32,2,48,128]{3,2,1,0:T(8,128)(2,1)}), bf16[32,2,48,128]{3,2,1,0:T(8,128)(2,1)S(1)}, u32[]{:S(2)}, u32[]{:S(2)}) %all-to-all-start) | async-done | bytes 786464 | tf_op jit(solution)/shard_map/all_to_all | solution.py:445
  76.1 2.0 %beams.1 = bf16[8,64,384]{2,1,0:T(8,128)(2,1)} custom-call(bf16[4,8,2,48,128]{4,3,2,1,0:T(8,128)(2,1)S(1)} %bitcast.10, bf16[2,512,1024]{2,1,0:T(8,128)(2,1)S(1)} %get-tuple-element.5.table_ref), custom_call_target="tpu_custom_call" | custom-call | tf_op jit(solution)/shard_map/beams/pallas_call | solution.py:383
  78.1 3.6 %all-to-all-start.1 = ((bf16[8,64,384]{2,1,0:T(8,128)(2,1)}), bf16[8,64,384]{2,1,0:T(8,128)(2,1)S(1)}, u32[]{:S(2)}, u32[]{:S(2)}) async-start(bf16[8,64,384]{2,1,0:T(8,128)(2,1)} %beams.1), calls=%async_computation.1 | async-start | bytes 786432 | tf_op jit(solution)/shard_map/all_to_all | solution.py:454
  81.8 0.0 copy-start.4
  81.8 1.6 %copy-done.4 = bf16[1024,1024]{1,0:T(8,128)(2,1)S(1)} copy-done((bf16[1024,1024]{1,0:T(8,128)(2,1)S(1)}, bf16[1024,1024]{1,0:T(8,128)(2,1)}, u32[]{:S(2)}) %copy-start.4) | copy-done | bytes 2097176
  83.4 7.2 %visibilities.1 = f32[1,2,1024,1024]{3,2,1,0:T(8,128)} custom-call(bf16[4,8,2,48,128]{4,3,2,1,0:T(8,128)(2,1)S(1)} %bitcast.11, bf16[1024,1024]{1,0:T(8,128)(2,1)S(1)} %copy-done.4), custom_call_target="tpu_custom_call" | custom-call | flops 3221225472 | bytes 8388608 | tf_op jit(solution)/shard_map/visibilities/pallas_call | solution.py:415
  90.6 2.7 %all-to-all-done.1 = bf16[8,64,384]{2,1,0:T(8,128)(2,1)S(1)} async-done(((bf16[8,64,384]{2,1,0:T(8,128)(2,1)}), bf16[8,64,384]{2,1,0:T(8,128)(2,1)S(1)}, u32[]{:S(2)}, u32[]{:S(2)}) %all-to-all-start.1) | async-done | bytes 393248 | tf_op jit(solution)/shard_map/all_to_all | solution.py:454
  93.3 0.1 convert_bitcast_fusion
  93.4 0.8 reshape.35
  94.1 1.6 %copy.10 = f32[64,8,2,192]{3,2,1,0:T(2,128)} copy(f32[64,8,2,192]{3,2,0,1:T(2,128)S(1)} %reshape.35) | data formatting | bytes 1572864
Async XLA Ops:
  0.6 53.5 %copy-start.5 = (s32[32]{0:T(128)S(1)}, s32[32]{0:T(128)}, u32[]{:S(2)}) copy-start(s32[32]{0:T(128)} %bins_ref.1) | copy-start | bytes 388
  0.6 54.8 %copy-start.1 = (s32[1024]{0:T(1024)S(1)}, s32[1024]{0:T(1024)}, u32[]{:S(2)}) copy-start(s32[1024]{0:T(1024)} %param.10) | copy-start | bytes 12292
  0.7 54.8 %copy-start.2 = (s32[512]{0:T(512)S(1)}, s32[512]{0:T(512)}, u32[]{:S(2)}) copy-start(s32[512]{0:T(512)} %param.11) | copy-start | bytes 6148
  46.8 29.3 %all-to-all-start = ((bf16[32,2,48,128]{3,2,1,0:T(8,128)(2,1)}), bf16[32,2,48,128]{3,2,1,0:T(8,128)(2,1)S(1)}, u32[]{:S(2)}, u32[]{:S(2)}) async-start(bf16[32,2,48,128]{3,2,1,0:T(8,128)(2,1)} %bitcast.14), calls=%async_computation | async-start | bytes 1572864 | tf_op jit(solution)/shard_map/all_to_all | solution.py:445
  55.4 1.6 %copy-start = (f32[512,1024]{1,0:T(8,128)S(1)}, f32[512,1024]{1,0:T(8,128)}, u32[]{:S(2)}) copy-start(f32[512,1024]{1,0:T(8,128)} %delays_ref.1) | copy-start | bytes 6291460
  63.8 1.3 %copy-start.3 = (bf16[1024,1024]{1,0:T(8,128)(2,1)}, bf16[1024,1024]{1,0:T(8,128)(2,1)S(1)}, u32[]{:S(2)}) copy-start(bf16[1024,1024]{1,0:T(8,128)(2,1)S(1)} %get-tuple-element.4.place_ref) | copy-start | bytes 6291460
  78.1 15.2 %all-to-all-start.1 = ((bf16[8,64,384]{2,1,0:T(8,128)(2,1)}), bf16[8,64,384]{2,1,0:T(8,128)(2,1)S(1)}, u32[]{:S(2)}, u32[]{:S(2)}) async-start(bf16[8,64,384]{2,1,0:T(8,128)(2,1)} %beams.1), calls=%async_computation.1 | async-start | bytes 786432 | tf_op jit(solution)/shard_map/all_to_all | solution.py:454
  81.8 1.6 %copy-start.4 = (bf16[1024,1024]{1,0:T(8,128)(2,1)S(1)}, bf16[1024,1024]{1,0:T(8,128)(2,1)}, u32[]{:S(2)}) copy-start(bf16[1024,1024]{1,0:T(8,128)(2,1)} %copy-done.3) | copy-start | bytes 6291460

commit v4 on v3

--- a/solution.py
+++ b/solution.py
@@ -432,6 +432,27 @@
     )(moved, place)
 
 
+def place_kernel(turned_ref, out_ref):
+    times = out_ref.shape[3]
+    for channel in range(out_ref.shape[1]):
+        values = turned_ref[channel].astype(jnp.float32)
+        for part in range(2):
+            out_ref[:, channel, part, :] = values[:, part * times : (part + 1) * times]
+
+
+def placed_beams(turned, times):
+    channels, beams, _ = turned.shape
+    vmem = pl.BlockSpec(memory_space=pltpu.VMEM)
+    return pl.pallas_call(
+        place_kernel,
+        in_specs=[vmem],
+        out_specs=vmem,
+        out_shape=jax.ShapeDtypeStruct((beams, channels, 2, times), jnp.float32),
+        compiler_params=pltpu.CompilerParams(vmem_limit_bytes=32 << 20),
+        name="place_beams",
+    )(turned)
+
+
 def body(voltages, chan_bins, antenna_map, beam_index, delays):
     signals_dev = voltages.shape[1]
     frames = voltages.shape[2] // NFFT - TAPS + 1
@@ -453,8 +474,7 @@
     formed = beams_of(moved, table, freq_count, times)
     turned = lax.all_to_all(formed, "freq", split_axis=0, concat_axis=0, tiled=True)
     visibilities = visibilities_of(moved, place, times)
-    turned = turned.transpose(1, 0, 2).astype(jnp.float32)
-    return (visibilities, turned.reshape(turned.shape[0], turned.shape[1], 2, times))
+    return (visibilities, placed_beams(turned, times))
 
 
 def solution(mesh):

time: 96.1 us -> 95.2 us (level)
  local copies, waits for them, and re-layouts: 7.4 us -> 5.09 us
  Pallas kernels: 62.2 us -> 63.7 us
    unnamed x13 -> x12, local copies, waits for them, and re-layouts: 6.06 us -> 4.5 us
    pallas_call x0 -> x1, Pallas kernels: none -> 1.54 us  [placed_beams(): pl.pallas_call(place_kernel, in_specs=[vmem], out_specs=vmem, out_shape=j...]
where the time goes in v4:
time: 95.2 us; the launch traced here: 94.9 us
  Pallas kernels  63.7 us (67%)
  waiting for transfers between devices  13.7 us (14%)
  starting transfers between devices  10.9 us (11%)
  local copies, waits for them, and re-layouts  5.09 us (5%)
  between operations  1.39 us (1%)
    pallas_call x1, Pallas kernels, spectra_of(): pl.pallas_call(functools.partial(spectra_kernel, chunk, frames, width, si...  46.2 us
    all_to_all x1, waiting for transfers between devices, body(): lax.all_to_all(spectra, ('tm', 'freq'), split_axis=0, concat_axis=0, tile...  11 us
    all_to_all x1, starting transfers between devices, body(): lax.all_to_all(spectra, ('tm', 'freq'), split_axis=0, concat_axis=0, tile...  7.3 us
    pallas_call x1, Pallas kernels, visibilities_of(): pl.pallas_call(visibility_kernel, grid=(antennas // rows,), in_specs=[pl....  7.21 us
    pallas_call x1, Pallas kernels, steering_of(): pl.pallas_call(steering_kernel, in_specs=[pl.BlockSpec(memory_space=pltpu...  6.76 us
    unnamed x12, local copies, waits for them, and re-layouts  4.5 us
    all_to_all x1, starting transfers between devices, body(): lax.all_to_all(formed, 'freq', split_axis=0, concat_axis=0, tiled=True)  3.63 us
    all_to_all x1, waiting for transfers between devices, body(): lax.all_to_all(formed, 'freq', split_axis=0, concat_axis=0, tiled=True)  2.73 us
  transfers between devices with their start and end apart: 2, of which 2 were waited for; matrix products, arithmetic and copies ran while one was open for 1% of the time, Pallas kernels for 15%

profile of v4, /device:TPU:0, one launch (start us, length us, event | category | flops | bytes accessed | tf_op | source)
XLA Modules:
  0.0 94.9 jit_solution(8086020598028984765)
XLA Ops:
  0.6 0.0 copy-start.5
  0.6 0.0 copy-start.1
  0.7 0.0 copy-start.2
  0.7 46.2 %spectra.1 = bf16[64,48,128]{2,1,0:T(8,128)(2,1)} custom-call(s32[32]{0:T(128)} %bins_ref.1, bf16[4096,128]{1,0:T(8,128)(2,1)} %constant.22.clone.basis_ref, f32[2,8,128]{2,1,0:T(8,128)} %constant.23.clone.mix_ref, bf16[2,8,16,128]{3,2,1,0:T(8,128)(2,1)} %constant.24.clone.minor_mix_ref, bf16[128,258048]{1,0:T(8,128)(2,1)} %bitcast.11), custom_call_target="tpu_custom_call" | custom-call | flops 33822867456 | bytes 66060288 | tf_op jit(solution)/shard_map/spectra/pallas_call | solution.py:263
  46.8 7.3 %all-to-all-start = ((bf16[32,2,48,128]{3,2,1,0:T(8,128)(2,1)}), bf16[32,2,48,128]{3,2,1,0:T(8,128)(2,1)S(1)}, u32[]{:S(2)}, u32[]{:S(2)}) async-start(bf16[32,2,48,128]{3,2,1,0:T(8,128)(2,1)} %bitcast.10), calls=%async_computation | async-start | bytes 1572864 | tf_op jit(solution)/shard_map/all_to_all | solution.py:466
  54.2 0.0 copy-done.5
  54.2 0.6 dynamic_slice.4
  55.4 0.0 copy-done.1
  55.4 0.0 copy-done.2
  55.4 0.0 copy-start
  55.4 1.6 %copy-done = f32[512,1024]{1,0:T(8,128)S(1)} copy-done((f32[512,1024]{1,0:T(8,128)S(1)}, f32[512,1024]{1,0:T(8,128)}, u32[]{:S(2)}) %copy-start) | copy-done | bytes 2097176
  57.0 6.8 %steering.1 = (bf16[2,512,1024]{2,1,0:T(8,128)(2,1)S(1)}, bf16[1024,1024]{1,0:T(8,128)(2,1)S(1)}) custom-call(f32[1,1]{1,0:T(1,128)} %bitcast.3.bin_ref, f32[512,1024]{1,0:T(8,128)S(1)} %copy-done, s32[1,512]{1,0:T(1,128)S(1)} %bitcast.9, s32[1,1024]{1,0:T(1,128)S(1)} %bitcast.8), custom_call_target="tpu_custom_call" | custom-call | flops 3242196992 | bytes 4194304 | tf_op jit(solution)/shard_map/steering/pallas_call | solution.py:335
  63.8 0.0 copy-start.3
  63.8 1.3 %copy-done.3 = bf16[1024,1024]{1,0:T(8,128)(2,1)} copy-done((bf16[1024,1024]{1,0:T(8,128)(2,1)}, bf16[1024,1024]{1,0:T(8,128)(2,1)S(1)}, u32[]{:S(2)}) %copy-start.3) | copy-done | bytes 2097176
  65.1 11.0 %all-to-all-done = bf16[32,2,48,128]{3,2,1,0:T(8,128)(2,1)S(1)} async-done(((bf16[32,2,48,128]{3,2,1,0:T(8,128)(2,1)}), bf16[32,2,48,128]{3,2,1,0:T(8,128)(2,1)S(1)}, u32[]{:S(2)}, u32[]{:S(2)}) %all-to-all-start) | async-done | bytes 786464 | tf_op jit(solution)/shard_map/all_to_all | solution.py:466
  76.1 2.0 %beams.1 = bf16[8,64,384]{2,1,0:T(8,128)(2,1)} custom-call(bf16[4,8,2,48,128]{4,3,2,1,0:T(8,128)(2,1)S(1)} %bitcast.6, bf16[2,512,1024]{2,1,0:T(8,128)(2,1)S(1)} %get-tuple-element.5.table_ref), custom_call_target="tpu_custom_call" | custom-call | tf_op jit(solution)/shard_map/beams/pallas_call | solution.py:383
  78.1 3.6 %all-to-all-start.1 = ((bf16[8,64,384]{2,1,0:T(8,128)(2,1)}), bf16[8,64,384]{2,1,0:T(8,128)(2,1)S(1)}, u32[]{:S(2)}, u32[]{:S(2)}) async-start(bf16[8,64,384]{2,1,0:T(8,128)(2,1)} %beams.1), calls=%async_computation.1 | async-start | bytes 786432 | tf_op jit(solution)/shard_map/all_to_all | solution.py:475
  81.8 0.0 copy-start.4
  81.8 1.6 %copy-done.4 = bf16[1024,1024]{1,0:T(8,128)(2,1)S(1)} copy-done((bf16[1024,1024]{1,0:T(8,128)(2,1)S(1)}, bf16[1024,1024]{1,0:T(8,128)(2,1)}, u32[]{:S(2)}) %copy-start.4) | copy-done | bytes 2097176
  83.4 7.2 %visibilities.1 = f32[1,2,1024,1024]{3,2,1,0:T(8,128)} custom-call(bf16[4,8,2,48,128]{4,3,2,1,0:T(8,128)(2,1)S(1)} %bitcast.7, bf16[1024,1024]{1,0:T(8,128)(2,1)S(1)} %copy-done.4), custom_call_target="tpu_custom_call" | custom-call | flops 3221225472 | bytes 8388608 | tf_op jit(solution)/shard_map/visibilities/pallas_call | solution.py:415
  90.6 2.7 %all-to-all-done.1.turned_ref = bf16[8,64,384]{2,1,0:T(8,128)(2,1)S(1)} async-done(((bf16[8,64,384]{2,1,0:T(8,128)(2,1)}), bf16[8,64,384]{2,1,0:T(8,128)(2,1)S(1)}, u32[]{:S(2)}, u32[]{:S(2)}) %all-to-all-start.1) | async-done | bytes 393248 | tf_op jit(solution)/shard_map/all_to_all | solution.py:475
  93.3 1.5 %place_beams.1 = f32[64,8,2,192]{3,2,1,0:T(2,128)} custom-call(bf16[8,64,384]{2,1,0:T(8,128)(2,1)S(1)} %all-to-all-done.1.turned_ref), custom_call_target="tpu_custom_call" | custom-call | tf_op jit(solution)/shard_map/place_beams/pallas_call | solution.py:446
Async XLA Ops:
  0.6 53.5 %copy-start.5 = (s32[32]{0:T(128)S(1)}, s32[32]{0:T(128)}, u32[]{:S(2)}) copy-start(s32[32]{0:T(128)} %bins_ref.1) | copy-start | bytes 388
  0.6 54.8 %copy-start.1 = (s32[1024]{0:T(1024)S(1)}, s32[1024]{0:T(1024)}, u32[]{:S(2)}) copy-start(s32[1024]{0:T(1024)} %param.10) | copy-start | bytes 12292
  0.7 54.8 %copy-start.2 = (s32[512]{0:T(512)S(1)}, s32[512]{0:T(512)}, u32[]{:S(2)}) copy-start(s32[512]{0:T(512)} %param.11) | copy-start | bytes 6148
  46.8 29.3 %all-to-all-start = ((bf16[32,2,48,128]{3,2,1,0:T(8,128)(2,1)}), bf16[32,2,48,128]{3,2,1,0:T(8,128)(2,1)S(1)}, u32[]{:S(2)}, u32[]{:S(2)}) async-start(bf16[32,2,48,128]{3,2,1,0:T(8,128)(2,1)} %bitcast.10), calls=%async_computation | async-start | bytes 1572864 | tf_op jit(solution)/shard_map/all_to_all | solution.py:466
  55.4 1.6 %copy-start = (f32[512,1024]{1,0:T(8,128)S(1)}, f32[512,1024]{1,0:T(8,128)}, u32[]{:S(2)}) copy-start(f32[512,1024]{1,0:T(8,128)} %delays_ref.1) | copy-start | bytes 6291460
  63.8 1.3 %copy-start.3 = (bf16[1024,1024]{1,0:T(8,128)(2,1)}, bf16[1024,1024]{1,0:T(8,128)(2,1)S(1)}, u32[]{:S(2)}) copy-start(bf16[1024,1024]{1,0:T(8,128)(2,1)S(1)} %get-tuple-element.4.place_ref) | copy-start | bytes 6291460
  78.1 15.2 %all-to-all-start.1 = ((bf16[8,64,384]{2,1,0:T(8,128)(2,1)}), bf16[8,64,384]{2,1,0:T(8,128)(2,1)S(1)}, u32[]{:S(2)}, u32[]{:S(2)}) async-start(bf16[8,64,384]{2,1,0:T(8,128)(2,1)} %beams.1), calls=%async_computation.1 | async-start | bytes 786432 | tf_op jit(solution)/shard_map/all_to_all | solution.py:475
  81.8 1.6 %copy-start.4 = (bf16[1024,1024]{1,0:T(8,128)(2,1)S(1)}, bf16[1024,1024]{1,0:T(8,128)(2,1)}, u32[]{:S(2)}) copy-start(bf16[1024,1024]{1,0:T(8,128)(2,1)} %copy-done.3) | copy-start | bytes 6291460
